TPU v7x, 256 devices: a whole 4x4x8 slice. The times are simulated.
256 devices in a mesh: section: 8 (over z_lo, core), ctx: 32 (over z_hi, x, y).
Axes of the slice: x: 4, y: 4, z: 8 (z_hi: 2, z_lo: 4; z = z_hi * 4 + z_lo), core: 2. Of those that a mesh axis runs over, the one named last changes fastest.
Arguments:
- section_input: bfloat16 [8, 1536, 8192], P('section', None, 'ctx'), may hold values from -6 to 6
- out_cotangent: bfloat16 [8, 1536, 2048], P('section', None, 'ctx'), may hold values from -96 to 96
- conv_weight: bfloat16 [8, 2, 1536, 640], P('section'), may hold values from -0.25 to 0.25
- norm_gain: float32 [8, 2, 1536], P('section'), may hold values from 0.1 to 1.9
Outputs:
- section_output: bfloat16 [8, 1536, 2048], P('section', None, 'ctx')
- input_grad: bfloat16 [8, 1536, 8192], P('section', None, 'ctx')
- weight_grad: float32 [8, 2, 1536, 640], P('section', None, 'ctx')
- gain_grad: float32 [8, 2, 1536], P('section', None, 'ctx')
All inputs are finite; a program needn't handle non-finite values.
Results may differ from a plain program's by a relative error of at most 0.02.
Values may be sent and summed in bfloat16 or wider, within the bound.
A program may use at most 128 MiB of HBM per device.

v0:
```python
import jax
import jax.numpy as jnp
from jax import lax
from jax.sharding import PartitionSpec as P


def extended(x, sides, width):
    for axis, dim in sides:
        size, length = (lax.axis_size(axis), x.shape[dim])
        up = [(i, (i + 1) % size) for i in range(size - 1)]
        down = [(j, i) for i, j in up]
        last = lax.slice_in_dim(x, length - width, length, axis=dim)
        first = lax.slice_in_dim(x, 0, width, axis=dim)
        before = lax.ppermute(last, axis, up)
        after = lax.ppermute(first, axis, down)
        x = jnp.concatenate([before, x, after], axis=dim)
    return x


def mirror(panel):
    spread = lax.all_to_all(panel, "ctx", split_axis=0, concat_axis=1, tiled=True)
    return lax.all_to_all(spread[:, ::-1], "ctx", split_axis=1, concat_axis=0, tiled=True)


def group_conv(padded, weight, length):
    channels = padded.shape[0]
    width = weight.shape[1] // 5
    groups = channels // width
    grouped = padded.reshape(groups, width, length + 4)
    stacked = jnp.concatenate(
        [grouped[:, :, offset : offset + length] for offset in range(5)], axis=1
    )
    wgroup = weight.reshape(groups, width, 5 * width)
    result = jnp.einsum("gok,gkp->gop", wgroup, stacked, preferred_element_type=jnp.float32)
    return (result.reshape(channels, length), stacked)


def forward_block(acts, weight, gain):
    channels, length = acts.shape
    halfway = channels // 2
    source = acts.astype(jnp.float32)
    inverse = lax.rsqrt(jnp.mean(source * source, axis=0, keepdims=True) + 1e-06)
    normed_raw = source * inverse
    normed = (normed_raw * gain[:, None]).astype(jnp.bfloat16)
    mirrored = mirror(normed[halfway:])
    mixed = (normed[:halfway].astype(jnp.float32) + mirrored.astype(jnp.float32)).astype(
        jnp.bfloat16
    )
    inputs = jnp.concatenate([mixed, normed[halfway:]], axis=0)
    padded = extended(inputs, (("ctx", 1),), 2)
    pre_act, stacked = group_conv(padded, weight, length)
    resid = source + jax.nn.gelu(pre_act)
    output = (0.5 * (resid[:, 0::2] + resid[:, 1::2])).astype(jnp.bfloat16)
    return (output, (normed_raw, inverse, pre_act, stacked))


def backward_block(grad_out, weight, gain, saved):
    normed_raw, inverse, pre_act, stacked = saved
    channels, length = normed_raw.shape
    halfway = channels // 2
    width = weight.shape[1] // 5
    groups = channels // width
    grad_res = jnp.repeat(grad_out, 2, axis=1) * 0.5
    unused, gelu_back = jax.vjp(jax.nn.gelu, pre_act)
    grad_pre = gelu_back(grad_res)[0].astype(jnp.bfloat16)
    pre_group = grad_pre.reshape(groups, width, length)
    wgrad = jnp.einsum(
        "gop,gkp->gok", pre_group, stacked, preferred_element_type=jnp.float32
    ).reshape(channels, 5 * width)
    padded = extended(grad_pre, (("ctx", 1),), 2).reshape(groups, width, length + 4)
    shifted = jnp.stack(
        [padded[:, :, 4 - offset : 4 - offset + length] for offset in range(5)], axis=1
    )
    wfour = weight.reshape(groups, width, 5, width)
    grad_mixed = (
        jnp.einsum("goki,gkop->gip", wfour, shifted, preferred_element_type=jnp.float32)
        .reshape(channels, length)
        .astype(jnp.bfloat16)
    )
    back = mirror(grad_mixed[:halfway])
    grad_norm = jnp.concatenate(
        [
            grad_mixed[:halfway].astype(jnp.float32),
            grad_mixed[halfway:].astype(jnp.float32) + back.astype(jnp.float32),
        ],
        axis=0,
    )
    ggrad = jnp.sum(grad_norm * normed_raw, axis=1)
    scaled = grad_norm * gain[:, None]
    grad_in = (
        scaled - normed_raw * jnp.mean(scaled * normed_raw, axis=0, keepdims=True)
    ) * inverse + grad_res
    return (grad_in, wgrad, ggrad)


def local(section_input, out_cotangent, conv_weight, norm_gain):
    acts = section_input[0]
    weights = conv_weight[0]
    gains = norm_gain[0]
    first, saved_one = forward_block(acts, weights[0], gains[0])
    second, saved_two = forward_block(first, weights[1], gains[1])
    grad_mid, wgrad_two, ggrad_two = backward_block(
        out_cotangent[0].astype(jnp.float32), weights[1], gains[1], saved_two
    )
    grad_in, wgrad_one, ggrad_one = backward_block(grad_mid, weights[0], gains[0], saved_one)
    wgrads = jnp.stack([wgrad_one, wgrad_two])
    ggrads = jnp.stack([ggrad_one, ggrad_two])
    count = lax.axis_size("section") * (wgrads.size + ggrads.size)
    wshare, gshare = (
        lax.psum_scatter(
            wgrads.astype(jnp.bfloat16), "ctx", scatter_dimension=1, tiled=True
        ).astype(jnp.float32),
        lax.psum_scatter(
            ggrads.astype(jnp.bfloat16), "ctx", scatter_dimension=1, tiled=True
        ).astype(jnp.float32),
    )
    local_square = jnp.sum(wshare * wshare) + jnp.sum(gshare * gshare)
    total = lax.psum(local_square, ("section", "ctx"))
    factor = jnp.minimum(1.0, lax.rsqrt(total / count + 1e-06))
    return (
        second[None],
        grad_in.astype(jnp.bfloat16)[None],
        (wshare * factor)[None],
        (gshare * factor)[None],
    )


def solution(mesh):
    placed = (
        P("section", None, "ctx"),
        P("section", None, "ctx"),
        P("section", None, None, None),
        P("section", None, None),
    )
    return jax.shard_map(
        local,
        mesh=mesh,
        in_specs=placed,
        out_specs=(
            P("section", None, "ctx"),
            P("section", None, "ctx"),
            P("section", None, "ctx", None),
            P("section", None, "ctx"),
        ),
        check_vma=False,
    )
```

profile of v0, /device:TPU:1, one launch (start us, length us, event | category | flops | bytes accessed | tf_op | source)
XLA Modules:
  0.0 1016.1 jit_solution(14867052209892291998)
XLA Ops:
  7.2 1.4 fusion.13
  9.4 1.4 fusion.10
  10.8 27.0 %all_to_all.128 = bf16[32,24,256]{2,1,0:T(8,128)(2,1)S(1)} all-to-all(bf16[32,24,256]{2,1,0:T(8,128)(2,1)S(1)} %bitcast.288), channel_id=1, replica_groups=mesh['section'=8,'ctx'=32] {'ctx'}, dimensions={0} | all-to-all | bytes 786432 | tf_op jit(solution)/shard_map/all_to_all | solution.py:21
  37.8 5.3 rev.12
  43.1 16.7 %all_to_all.129 = bf16[24,32,256]{2,0,1:T(8,128)(2,1)S(1)} all-to-all(bf16[24,32,256]{2,0,1:T(8,128)(2,1)S(1)} %bitcast.299), channel_id=1, replica_groups=mesh['section'=8,'ctx'=32] {'ctx'}, dimensions={1} | all-to-all | bytes 786432 | tf_op jit(solution)/shard_map/all_to_all | solution.py:22
  60.1 2.2 collective-permute-start
  62.4 1.3 collective-permute-start.1
  64.0 3.0 collective-permute-done
  67.1 3.8 collective-permute-done.1
  74.9 1.2 copy-done.2
  76.0 1.8 fusion.4
  77.8 28.4 %slice.160 = f32[1536,128]{1,0:T(8,128)} slice(f32[1536,256]{1,0:T(8,128)} %fusion.4), slice={[0:1536:1], [1:256:2]} | slice | bytes 1572864 | tf_op jit(solution)/shard_map/slice | solution.py:53
  106.1 28.3 %slice.159 = f32[1536,128]{1,0:T(8,128)} slice(f32[1536,256]{1,0:T(8,128)} %fusion.4), slice={[0:1536:1], [0:256:2]} | slice | bytes 1572864 | tf_op jit(solution)/shard_map/slice | solution.py:53
  134.5 1.6 fusion.76
  137.6 26.4 %all_to_all.130 = bf16[32,24,128]{2,1,0:T(8,128)(2,1)S(1)} all-to-all(bf16[32,24,128]{2,1,0:T(8,128)(2,1)S(1)} %bitcast.290), channel_id=1, replica_groups=mesh['section'=8,'ctx'=32] {'ctx'}, dimensions={0} | all-to-all | bytes 393216 | tf_op jit(solution)/shard_map/all_to_all | solution.py:21
  164.0 10.8 %rev.13 = bf16[24,4096]{1,0:T(8,128)(2,1)} reverse(bf16[24,4096]{1,0:T(8,128)(2,1)S(1)} %copy_bitcast_fusion.3), dimensions={1} | reverse | bytes 393216 | tf_op jit(solution)/shard_map/rev | solution.py:22
  175.8 14.9 %all_to_all.131 = bf16[24,32,128]{2,0,1:T(8,128)(2,1)S(1)} all-to-all(bf16[24,32,128]{2,0,1:T(8,128)(2,1)S(1)} %copy_bitcast_fusion.5), channel_id=1, replica_groups=mesh['section'=8,'ctx'=32] {'ctx'}, dimensions={1} | all-to-all | bytes 393216 | tf_op jit(solution)/shard_map/all_to_all | solution.py:22
  192.7 2.8 collective-permute-start.2
  195.5 1.7 collective-permute-start.3
  198.4 2.6 mul.377
  201.1 2.3 copy.99
  204.3 1.6 pad_maximum_fusion.4
  208.7 1.6 fusion.61
  211.4 3.8 collective-permute-start.4
  215.2 1.3 collective-permute-start.5
  216.5 3.5 reshape.236
  220.0 4.0 collective-permute-done.5
  224.0 1.6 pad_maximum_fusion.5
  228.3 32.6 %all_to_all.132 = bf16[32,24,128]{2,1,0:T(8,128)(2,1)S(1)} all-to-all(bf16[32,24,128]{2,1,0:T(8,128)(2,1)S(1)} %bitcast.292), channel_id=1, replica_groups=mesh['section'=8,'ctx'=32] {'ctx'}, dimensions={0} | all-to-all | bytes 393216 | tf_op jit(solution)/shard_map/all_to_all | solution.py:21
  260.9 2.6 rev.14
  264.3 7.4 all-to-all-start.5
  271.7 11.8 %all-to-all-done.5 = bf16[24,32,128]{2,0,1:T(8,128)(2,1)S(1)} async-done(((bf16[24,32,128]{2,0,1:T(8,128)(2,1)}), bf16[24,32,128]{2,0,1:T(8,128)(2,1)S(1)}, u32[]{:S(2)}, u32[]{:S(2)}) %all-to-all-start.5) | async-done | bytes 196640 | tf_op jit(solution)/shard_map/all_to_all | solution.py:22
  286.2 1.7 broadcast_in_dim.22
  287.8 2.3 mul.395
  290.1 3.1 copy.111
  293.2 2.9 fusion.25
  297.0 2.8 collective-permute-start.6
  299.8 1.3 collective-permute-start.7
  301.1 5.6 reshape.237
  306.7 1.7 collective-permute-done.7
  308.4 1.8 pad_maximum_fusion.3
  311.6 1.2 copy-done.4
  313.7 1.3 slice_convert_fusion
  315.0 13.7 %all-to-all-start.6 = ((bf16[32,24,256]{2,1,0:T(8,128)(2,1)}), bf16[32,24,256]{2,1,0:T(8,128)(2,1)S(1)}, u32[]{:S(2)}, u32[]{:S(2)}) async-start(bf16[32,24,256]{2,1,0:T(8,128)(2,1)} %bitcast.296), calls=%async_computation.6 | async-start | bytes 786432 | tf_op jit(solution)/shard_map/all_to_all | solution.py:21
  328.7 1.6 mul.432
  330.3 2.4 copy.124
  332.7 8.3 all-to-all-done.6
  341.8 24.7 %rev.15 = bf16[24,8192]{1,0:T(8,128)(2,1)S(1)} reverse(bf16[24,8192]{1,0:T(8,128)(2,1)} %bitcast.300), dimensions={1} | reverse | bytes 786432 | tf_op jit(solution)/shard_map/rev | solution.py:22
  367.3 4.0 all-to-all-start.7
  371.5 3.9 convolution_convert_fusion.1
  375.5 2.6 mul.417
  378.1 2.8 copy.122
  380.9 5.7 convolution_convert_fusion
  389.8 4.4 pad_maximum_fusion
  395.4 15.6 %slice.173 = f32[1536,64]{1,0:T(8,128)} slice(f32[1536,128]{1,0:T(8,128)S(1)} %copy-done.6), slice={[0:1536:1], [1:128:2]} | slice | bytes 786432 | tf_op jit(solution)/shard_map/slice | solution.py:53
  411.0 15.4 %slice.172 = f32[1536,64]{1,0:T(8,128)} slice(f32[1536,128]{1,0:T(8,128)S(1)} %copy-done.6), slice={[0:1536:1], [0:128:2]} | slice | bytes 786432 | tf_op jit(solution)/shard_map/slice | solution.py:53
  426.4 1.5 multiply_convert_fusion
  428.7 2.3 mul.416
  431.0 3.2 copy.121
  434.1 231.4 %reduce-scatter.7.cloned.1.call-done = bf16[48,2]{1,0:T(8,128)(2,1)} async-done(((bf16[1536,2]{1,0:T(8,128)(2,1)}), bf16[48,2]{1,0:T(8,128)(2,1)}) %reduce-scatter.7.cloned.1.call-update) | async-done | bytes 208
  666.9 260.9 %reduce-scatter.5.cloned.1.call-done = bf16[2,48,640]{2,1,0:T(8,128)(2,1)} async-done(((bf16[2,1536,640]{2,1,0:T(8,128)(2,1)}), bf16[2,48,640]{2,1,0:T(8,128)(2,1)}) %reduce-scatter.5.cloned.1.call-update) | async-done | bytes 122896 | tf_op jit(solution)/shard_map/reduce_scatter | solution.py:110
  927.8 1.6 fusion.108
  930.7 2.7 fusion.18
  933.5 73.6 %psum.7 = f32[]{:T(128)} all-reduce(f32[]{:T(128)S(6)} %add.117), channel_id=1, replica_groups=mesh['section'=8,'ctx'=32] {'section','ctx'}, use_global_device_ids=true, to_apply=%region_10.0 | all-reduce | flops 1 | bytes 8 | tf_op jit(solution)/shard_map/psum | solution.py:118
  (130 shorter events, 34.8 us)
Async XLA Ops:
  8.5 29.2 %copy-start.22 = (f32[256]{0:T(256)}, f32[256]{0:T(256)S(1)}, u32[]{:S(2)}) copy-start(f32[256]{0:T(256)S(1)} %add_rsqrt_fusion) | copy-start | bytes 3076
  43.1 20.6 %copy-start.16 = (bf16[1,2,1536,640]{3,2,1,0:T(8,128)(2,1)S(1)}, bf16[1,2,1536,640]{3,2,1,0:T(8,128)(2,1)}, u32[]{:S(2)}) copy-start(bf16[1,2,1536,640]{3,2,1,0:T(8,128)(2,1)} %param.6) | copy-start | bytes 11796484
  60.1 6.9 collective-permute-start
  62.4 8.5 collective-permute-start.1
  64.0 9.0 copy-start.1
  73.0 1.9 copy-start.15
  73.0 3.0 copy-start
  74.9 1.2 copy-start.2
  136.1 0.5 copy-start.25
  136.9 0.7 copy-start.18
  174.8 22.5 %copy-start.20 = (bf16[1,1536,64]{1,2,0:T(8,128)(2,1)S(1)}, bf16[1,1536,64]{1,2,0:T(8,128)(2,1)}, u32[]{:S(2)}) copy-start(bf16[1,1536,64]{1,2,0:T(8,128)(2,1)} %param.5) | copy-start | bytes 589828
  192.7 10.7 %collective-permute-start.2 = (bf16[1536,2]{1,0:T(8,128)(2,1)}, bf16[1536,2]{1,0:T(8,128)(2,1)}, u32[]{:S(2)}, u32[]{:S(2)}) collective-permute-start(bf16[1536,2]{1,0:T(8,128)(2,1)} %get-tuple-element.31), channel_id=1, source_target_pairs={{0,1},{1,2},{2,3},{3,4},{4,5},{5,6},{6,7},{7,8},{8,9},{9,10},{10,1... | collective-permute-start | bytes 18440 | tf_op jit(solution)/shard_map/ppermute | solution.py:14
  195.5 8.8 collective-permute-start.3
  207.0 1.3 copy-start.3
  207.0 1.7 copy-start.9
  208.7 1.6 copy-start.7
  211.4 8.6 collective-permute-start.4
  215.2 8.8 collective-permute-start.5
  225.6 1.9 copy-start.17
  263.6 20.0 %copy-start.26 = (f32[128]{0:T(128)S(1)}, f32[128]{0:T(128)}, u32[]{:S(2)}) copy-start(f32[128]{0:T(128)} %copy-done.25) | copy-start | bytes 1540
  264.3 19.2 %all-to-all-start.5 = ((bf16[24,32,128]{2,0,1:T(8,128)(2,1)}), bf16[24,32,128]{2,0,1:T(8,128)(2,1)S(1)}, u32[]{:S(2)}, u32[]{:S(2)}) async-start(bf16[24,32,128]{2,0,1:T(8,128)(2,1)} %copy_bitcast_fusion.4), calls=%async_computation.5 | async-start | bytes 393216 | tf_op jit(solution)/shard_map/all_to_all | solution.py:22
  271.7 13.0 %copy-start.10 = (f32[1536,128]{1,0:T(8,128)S(1)}, f32[1536,128]{1,0:T(8,128)}, u32[]{:S(2)}) copy-start(f32[1536,128]{1,0:T(8,128)} %copy.99) | copy-start | bytes 2359300
  297.0 9.7 collective-permute-start.6
  299.8 8.6 collective-permute-start.7
  310.9 1.9 copy-start.4
  313.7 15.0 %copy-start.5 = (f32[1536,64,2]{0,2,1:T(2,128)S(1)}, f32[1536,64,2]{0,2,1:T(2,128)}, u32[]{:S(2)}) copy-start(f32[1536,64,2]{0,2,1:T(2,128)} %broadcast_in_dim.21) | copy-start | bytes 2359300
  315.0 26.0 %all-to-all-start.6 = ((bf16[32,24,256]{2,1,0:T(8,128)(2,1)}), bf16[32,24,256]{2,1,0:T(8,128)(2,1)S(1)}, u32[]{:S(2)}, u32[]{:S(2)}) async-start(bf16[32,24,256]{2,1,0:T(8,128)(2,1)} %bitcast.296), calls=%async_computation.6 | async-start | bytes 786432 | tf_op jit(solution)/shard_map/all_to_all | solution.py:21
  341.0 30.5 %copy-start.8 = (f32[12,128,128]{1,2,0:T(8,128)S(1)}, f32[12,128,128]{1,2,0:T(8,128)}, u32[]{:S(2)}) copy-start(f32[12,128,128]{1,2,0:T(8,128)} %copy-done.7) | copy-start | bytes 2359300
  367.3 19.3 %all-to-all-start.7 = ((bf16[24,32,256]{2,0,1:T(8,128)(2,1)}), bf16[24,32,256]{2,0,1:T(8,128)(2,1)S(1)}, u32[]{:S(2)}, u32[]{:S(2)}) async-start(bf16[24,32,256]{2,0,1:T(8,128)(2,1)} %bitcast.260), calls=%async_computation.7 | async-start | bytes 786432 | tf_op jit(solution)/shard_map/all_to_all | solution.py:22
  371.3 294.3 %reduce-scatter.7.cloned.1.call-start = ((), (), s32[]{:S(2)}) async-start(), calls=%async_computation.11 | async-start | bytes 405504
  375.5 2.6 copy-start.21
  386.6 1.3 copy-start.11
  386.6 1.2 copy-start.23
  387.8 0.9 copy-start.13
  389.8 538.0 %reduce-scatter.5.cloned.1.call-start = ((), (), s32[]{:S(2)}) async-start(), calls=%async_computation.10 | async-start | bytes 4055040 | tf_op jit(solution)/shard_map/reduce_scatter | solution.py:110
  394.2 1.1 copy-start.6
  431.0 499.7 %copy-start.12 = (f32[6,128,256]{2,1,0:T(8,128)S(1)}, f32[6,128,256]{2,1,0:T(8,128)}, u32[]{:S(2)}) copy-start(f32[6,128,256]{2,1,0:T(8,128)} %get-tuple-element.18) | copy-start | bytes 2359300
  431.0 499.7 %copy-start.14 = (f32[768,256]{1,0:T(8,128)S(1)}, f32[768,256]{1,0:T(8,128)}, u32[]{:S(2)}) copy-start(f32[768,256]{1,0:T(8,128)} %copy-done.13) | copy-start | bytes 2359300
  431.0 499.7 %copy-start.24 = (f32[256]{0:T(256)S(1)}, f32[256]{0:T(256)}, u32[]{:S(2)}) copy-start(f32[256]{0:T(256)} %copy-done.22) | copy-start | bytes 3076
  930.7 77.6 %copy-start.19 = (bf16[2,48,640]{2,1,0:T(8,128)(2,1)S(1)}, bf16[2,48,640]{2,1,0:T(8,128)(2,1)}, u32[]{:S(2)}) copy-start(bf16[2,48,640]{2,1,0:T(8,128)(2,1)} %reduce-scatter.5.cloned.1.call-done) | copy-start | bytes 368644
Sparse Core Ops, SparseCore 0:
  389.9 275.6 reduce-scatter.6
  671.9 255.8 reduce-scatter.4
where the time goes:
time: 1030 us; the launch traced here: 1020 us
  waiting for transfers between devices  526 us (51%)
  local copies, waits for them, and re-layouts  191 us (19%)
  blocking collectives  191 us (19%)
  starting transfers between devices  42.6 us (4%)
  other arithmetic  35.6 us (3%)
  between operations  16.9 us (2%)
  matrix products  12.8 us (1%)
    reduce_scatter x1, waiting for transfers between devices, local(): lax.psum_scatter(wgrads.astype(jnp.bfloat16), 'ctx', scatter_dimension=1,...  261 us
    unnamed x3, waiting for transfers between devices  231 us
    slice x4, local copies, waits for them, and re-layouts, forward_block(): output = (0.5 * (resid[:, 0::2] + resid[:, 1::2])).astype(jnp.bfloat16)  87.7 us
    all_to_all x3, blocking collectives, mirror(): lax.all_to_all(panel, 'ctx', split_axis=0, concat_axis=1, tiled=True)  86 us
    psum x1, blocking collectives, local(): total = lax.psum(local_square, ('section', 'ctx'))  73.6 us
    rev x4, local copies, waits for them, and re-layouts, mirror(): spread[:, ::-1]  43.4 us
    all_to_all x2, blocking collectives, mirror(): lax.all_to_all(spread[:, ::-1], 'ctx', split_axis=1, concat_axis=0, tiled...  31.6 us
    mul x11, local copies, waits for them, and re-layouts, backward_block(): grad_res = jnp.repeat(grad_out, 2, axis=1) * 0.5  26.2 us
  transfers between devices with their start and end apart: 13, of which 9 were waited for; matrix products, arithmetic and copies ran while one was open for 8% of the time, Pallas kernels for 0%

commit v1 on v0

--- a/solution.py
+++ b/solution.py
@@ -1,7 +1,176 @@
 import jax
 import jax.numpy as jnp
 from jax import lax
+from jax.experimental import pallas as pl
+from jax.experimental.pallas import tpu as pltpu
 from jax.sharding import PartitionSpec as P
+
+MESH = pl.DeviceIdType.MESH
+F32 = jnp.float32
+BF16 = jnp.bfloat16
+COUNT = 15753216.0
+
+
+def reduce_kernel(w, dg, out, gout, ra, rb, pa, pb, qa, qb, sab, tz, gbuf, g1, g2, g3, sq, sq1, sq2,
+                  ss1, rs1, ss2, rs2, ss3, rs3, sg, rg, sn, rn):
+    sec = lax.axis_index("section")
+    me = lax.axis_index("ctx")
+    z = me // 16
+    x = (me // 4) % 4
+    y = me % 4
+    plane = me % 16
+    line = sec * 2 + z
+
+    def at_x(d):
+        return {"section": sec, "ctx": z * 16 + ((x + d) % 4) * 4 + y}
+
+    def at_y(d):
+        return {"section": sec, "ctx": z * 16 + x * 4 + (y + d) % 4}
+
+    def at_z():
+        return {"section": sec, "ctx": (1 - z) * 16 + plane}
+
+    def at_plane(d):
+        return {"section": sec, "ctx": z * 16 + (plane + d) % 16}
+
+    def at_line(d):
+        other = (line + d) % 16
+        return {"section": other // 2, "ctx": (other % 2) * 16 + plane}
+
+    def copy(src, dst, send, recv, device):
+        return pltpu.make_async_remote_copy(
+            src_ref=src, dst_ref=dst, send_sem=send, recv_sem=recv,
+            device_id=device, device_id_type=MESH)
+
+    barrier = pltpu.get_barrier_semaphore()
+    for d in range(1, 16):
+        pl.semaphore_signal(barrier, inc=1, device_id=at_plane(d), device_id_type=MESH)
+        pl.semaphore_signal(barrier, inc=1, device_id=at_line(d), device_id_type=MESH)
+    pl.semaphore_wait(barrier, 30)
+
+    def first(b):
+        cps = []
+        for d in range(1, 4):
+            cps.append(copy(w.at[b, 0, (x + d) % 4], ra.at[b, d - 1],
+                            ss1.at[b, 0, d - 1], rs1.at[b, 0, d - 1], at_x(d)))
+            cps.append(copy(w.at[b, 1, :, (y + d) % 4], rb.at[b, d - 1],
+                            ss1.at[b, 1, d - 1], rs1.at[b, 1, d - 1], at_y(d)))
+        return cps
+
+    def second(b):
+        cps = []
+        for d in range(1, 4):
+            cps.append(copy(pa.at[b, (y + d) % 4], qa.at[b, d - 1],
+                            ss2.at[b, 0, d - 1], rs2.at[b, 0, d - 1], at_y(d)))
+            cps.append(copy(pb.at[b, (x + d) % 4], qb.at[b, d - 1],
+                            ss2.at[b, 1, d - 1], rs2.at[b, 1, d - 1], at_x(d)))
+        return cps
+
+    def third(b):
+        return copy(sab.at[b, 1 - z], tz.at[b], ss3.at[b], rs3.at[b], at_z())
+
+    def add_first(b):
+        @pl.loop(0, 4)
+        def _(k):
+            a = w[b, 0, x, k].astype(F32)
+            c = w[b, 1, k, y].astype(F32)
+            for d in range(3):
+                a += ra[b, d, k].astype(F32)
+                c += rb[b, d, k].astype(F32)
+            pa[b, k] = a.astype(BF16)
+            pb[b, k] = c.astype(BF16)
+
+    def add_second(b):
+        a = pa[b, y].astype(F32)
+        c = pb[b, x].astype(F32)
+        for d in range(3):
+            a += qa[b, d].astype(F32)
+            c += qb[b, d].astype(F32)
+        sab[b, 0] = a.astype(BF16)
+        sab[b, 1] = c.astype(BF16)
+
+    order = (1, 0)
+    for b in order:
+        for cp in first(b):
+            cp.start()
+    gbuf[0] = dg[...]
+    gx = [copy(gbuf.at[0], g1.at[d - 1], sg.at[0, d - 1], rg.at[0, d - 1], at_x(d)) for d in range(1, 4)]
+    for cp in gx:
+        cp.start()
+    for cp in gx:
+        cp.wait()
+    gbuf[1] = gbuf[0] + g1[0] + g1[1] + g1[2]
+    gy = [copy(gbuf.at[1], g2.at[d - 1], sg.at[1, d - 1], rg.at[1, d - 1], at_y(d)) for d in range(1, 4)]
+    for cp in gy:
+        cp.start()
+    for b in order:
+        for cp in first(b):
+            cp.wait()
+        add_first(b)
+        for cp in second(b):
+            cp.start()
+    for cp in gy:
+        cp.wait()
+    gbuf[2] = gbuf[1] + g2[0] + g2[1] + g2[2]
+    gz = copy(gbuf.at[2], g3, sg.at[2, 0], rg.at[2, 0], at_z())
+    gz.start()
+    for b in order:
+        for cp in second(b):
+            cp.wait()
+        add_second(b)
+        third(b).start()
+    gz.wait()
+    total_g = gbuf[2] + g3[...]
+    square = jnp.sum(total_g * total_g) * (1.0 / 32.0)
+    for b in order:
+        third(b).wait()
+        full = sab[b, z].astype(F32) + tz[b].astype(F32)
+        out[b] = full
+        square += jnp.sum(full * full)
+    sq[0] = jnp.full((8, 128), square, F32)
+    near = [copy(sq.at[0], sq1.at[d - 1], sn.at[0, d - 1], rn.at[0, d - 1], at_plane(d)) for d in range(1, 16)]
+    for cp in near:
+        cp.start()
+    for cp in near:
+        cp.wait()
+    sq[1] = sq[0] + jnp.sum(sq1[...], axis=0)
+    far = [copy(sq.at[1], sq2.at[d - 1], sn.at[1, d - 1], rn.at[1, d - 1], at_line(d)) for d in range(1, 16)]
+    for cp in far:
+        cp.start()
+    for cp in far:
+        cp.wait()
+    total = sq[1] + jnp.sum(sq2[...], axis=0)
+    factor = jnp.minimum(1.0, lax.rsqrt(total / COUNT + 1e-06))[0:1, 0:1]
+    for b in range(2):
+        out[b] = out[b] * factor
+    gout[...] = total_g * factor
+
+
+def reduce_gradients(wgrads, ggrads):
+    w = wgrads.astype(BF16).reshape(2, 2, 4, 4, 48, 640)
+    dg = jnp.concatenate([ggrads.reshape(24, 128), jnp.zeros((8, 128), F32)])
+    panel = pltpu.VMEM((2, 3, 4, 48, 640), BF16)
+    dma = pltpu.SemaphoreType.DMA
+    return pl.pallas_call(
+        reduce_kernel,
+        out_shape=(jax.ShapeDtypeStruct((2, 48, 640), F32), jax.ShapeDtypeStruct((32, 128), F32)),
+        in_specs=[pl.BlockSpec(memory_space=pltpu.VMEM)] * 2,
+        out_specs=[pl.BlockSpec(memory_space=pltpu.VMEM)] * 2,
+        scratch_shapes=[
+            panel, panel,
+            pltpu.VMEM((2, 4, 48, 640), BF16), pltpu.VMEM((2, 4, 48, 640), BF16),
+            pltpu.VMEM((2, 3, 48, 640), BF16), pltpu.VMEM((2, 3, 48, 640), BF16),
+            pltpu.VMEM((2, 2, 48, 640), BF16), pltpu.VMEM((2, 48, 640), BF16),
+            pltpu.VMEM((3, 32, 128), F32), pltpu.VMEM((3, 32, 128), F32),
+            pltpu.VMEM((3, 32, 128), F32), pltpu.VMEM((32, 128), F32),
+            pltpu.VMEM((2, 8, 128), F32), pltpu.VMEM((15, 8, 128), F32), pltpu.VMEM((15, 8, 128), F32),
+            dma((2, 2, 3)), dma((2, 2, 3)), dma((2, 2, 3)), dma((2, 2, 3)), dma((2,)), dma((2,)),
+            dma((3, 3)), dma((3, 3)), dma((2, 15)), dma((2, 15)),
+        ],
+        compiler_params=pltpu.CompilerParams(
+            collective_id=0, has_side_effects=True, vmem_limit_bytes=48 << 20),
+        name="reduce_gradients",
+    )(w, dg)
 
 
 def extended(x, sides, width):
@@ -18,8 +187,9 @@
 
 
 def mirror(panel):
-    spread = lax.all_to_all(panel, "ctx", split_axis=0, concat_axis=1, tiled=True)
-    return lax.all_to_all(spread[:, ::-1], "ctx", split_axis=1, concat_axis=0, tiled=True)
+    size = lax.axis_size("ctx")
+    pairs = [(i, size - 1 - i) for i in range(size)]
+    return lax.ppermute(panel[:, ::-1], "ctx", pairs)
 
 
 def group_conv(padded, weight, length):
@@ -105,23 +275,14 @@
     grad_in, wgrad_one, ggrad_one = backward_block(grad_mid, weights[0], gains[0], saved_one)
     wgrads = jnp.stack([wgrad_one, wgrad_two])
     ggrads = jnp.stack([ggrad_one, ggrad_two])
-    count = lax.axis_size("section") * (wgrads.size + ggrads.size)
-    wshare, gshare = (
-        lax.psum_scatter(
-            wgrads.astype(jnp.bfloat16), "ctx", scatter_dimension=1, tiled=True
-        ).astype(jnp.float32),
-        lax.psum_scatter(
-            ggrads.astype(jnp.bfloat16), "ctx", scatter_dimension=1, tiled=True
-        ).astype(jnp.float32),
-    )
-    local_square = jnp.sum(wshare * wshare) + jnp.sum(gshare * gshare)
-    total = lax.psum(local_square, ("section", "ctx"))
-    factor = jnp.minimum(1.0, lax.rsqrt(total / count + 1e-06))
+    wshare, gfull = reduce_gradients(wgrads, ggrads)
+    me = lax.axis_index("ctx")
+    gshare = lax.dynamic_slice(gfull[:24].reshape(2, 1536), (0, me * 48), (2, 48))
     return (
         second[None],
         grad_in.astype(jnp.bfloat16)[None],
-        (wshare * factor)[None],
-        (gshare * factor)[None],
+        wshare[None],
+        gshare[None],
     )
 
 

time: 1030 us -> 299 us (0.29); the launches traced: 1020 us -> 298 us
  waiting for transfers between devices: 526 us -> 26 us
  blocking collectives: 191 us -> 0 us
  local copies, waits for them, and re-layouts: 191 us -> 71.4 us
  Pallas kernels: 0 us -> 98.3 us
  starting transfers between devices: 42.6 us -> 67 us
  between operations: 16.9 us -> 1.34 us
  other arithmetic: 35.6 us -> 20.7 us
    reduce_scatter x1 -> x0, waiting for transfers between devices: 261 us -> none  [local(): lax.psum_scatter(wgrads.astype(jnp.bfloat16), 'ctx', scatter_dimension=1,...]
    unnamed x3 -> x0, waiting for transfers between devices: 231 us -> none
    all_to_all x5 -> x0, blocking collectives: 118 us -> none  [the longest x3 86 us: mirror(): lax.all_to_all(panel, 'ctx', split_axis=0, concat_axis=1, tiled=True)]
    pallas_call x0 -> x1, Pallas kernels: none -> 98.3 us  [reduce_gradients(): pl.pallas_call(reduce_kernel, out_shape=(jax.ShapeDtypeStruct((2, 48, 640...]
    slice x4, local copies, waits for them, and re-layouts: 87.7 us -> 11.8 us  [forward_block(): output = (0.5 * (resid[:, 0::2] + resid[:, 1::2])).astype(jnp.bfloat16)]
    psum x1 -> x0, blocking collectives: 73.6 us -> none  [local(): total = lax.psum(local_square, ('section', 'ctx'))]
    ppermute x0 -> x4, starting transfers between devices: none -> 47.2 us  [mirror(): return lax.ppermute(panel[:, ::-1], 'ctx', pairs)]
    rev x4, local copies, waits for them, and re-layouts: 43.4 us -> 1.46 us  [mirror(): return lax.ppermute(panel[:, ::-1], 'ctx', pairs)]
  transfers between devices with their start and end apart: 13 -> 12, of which waited for: 9 -> 4; matrix products, arithmetic and copies ran while one was open for 8% -> 13% of each run, Pallas kernels for 0% -> 0%
where the time goes in v1:
time: 299 us; the launch traced here: 298 us
  Pallas kernels  98.3 us (33%)
  local copies, waits for them, and re-layouts  71.4 us (24%)
  starting transfers between devices  67 us (22%)
  waiting for transfers between devices  26 us (9%)
  other arithmetic  20.7 us (7%)
  matrix products  13.3 us (4%)
    pallas_call x1, Pallas kernels, reduce_gradients(): pl.pallas_call(reduce_kernel, out_shape=(jax.ShapeDtypeStruct((2, 48, 640...  98.3 us
    ppermute x4, starting transfers between devices, mirror(): return lax.ppermute(panel[:, ::-1], 'ctx', pairs)  47.2 us
    ppermute x4, waiting for transfers between devices, mirror(): return lax.ppermute(panel[:, ::-1], 'ctx', pairs)  26 us
    unnamed x61, local copies, waits for them, and re-layouts  17.9 us
    mul x7, local copies, waits for them, and re-layouts, backward_block(): grad_res = jnp.repeat(grad_out, 2, axis=1) * 0.5  15.4 us
    ppermute x4, starting transfers between devices, extended(): before = lax.ppermute(last, axis, up)  14.4 us
    slice x4, local copies, waits for them, and re-layouts, forward_block(): output = (0.5 * (resid[:, 0::2] + resid[:, 1::2])).astype(jnp.bfloat16)  11.8 us
    another operation x2, local copies, waits for them, and re-layouts, backward_block(): wfour = weight.reshape(groups, width, 5, width)  9.24 us
  transfers between devices with their start and end apart: 12, of which 4 were waited for; matrix products, arithmetic and copies ran while one was open for 13% of the time, Pallas kernels for 0%

profile of v1, /device:TPU:1, one launch (start us, length us, event | category | flops | bytes accessed | tf_op | source)
XLA Modules:
  0.0 298.0 jit_solution(8591843978758637268)
XLA Ops:
  0.6 0.8 slice_reduce_fusion
  1.5 1.4 copy.17
  4.2 12.5 %collective-permute-start = (bf16[768,256]{0,1:T(8,128)(2,1)S(1)}, bf16[768,256]{0,1:T(8,128)(2,1)S(1)}, u32[]{:S(2)}, u32[]{:S(2)}) collective-permute-start(bf16[768,256]{0,1:T(8,128)(2,1)S(1)} %rev.12), channel_id=1, source_target_pairs={{0,31},{1,30},{2,29},{3,28},{4,27},{5,26},{6,25},{7,24},{8,23},{9,... | collective-permute-start | bytes 1179656 | tf_op jit(solution)/shard_map/ppermute | solution.py:192
  16.7 16.0 %collective-permute-done = bf16[768,256]{0,1:T(8,128)(2,1)S(1)} collective-permute-done((bf16[768,256]{0,1:T(8,128)(2,1)S(1)}, bf16[768,256]{0,1:T(8,128)(2,1)S(1)}, u32[]{:S(2)}, u32[]{:S(2)}) %collective-permute-start) | collective-permute-done | bytes 393248 | tf_op jit(solution)/shard_map/ppermute | solution.py:192
  32.8 1.8 collective-permute-start.1
  34.6 1.3 collective-permute-start.2
  35.9 4.5 %fusion.114 = (bf16[1,1,1536,640]{3,2,1,0:T(8,128)(2,1)}, bf16[1,1,1536,640]{3,2,1,0:T(8,128)(2,1)}) fusion(bf16[1,2,1536,640]{3,2,1,0:T(8,128)(2,1)} %param.6), kind=kLoop, calls=%fused_computation.170 | loop fusion | bytes 7864320 | tf_op jit(solution)/shard_map/slice | solution.py:271
  40.6 0.7 copy.18
  42.6 0.9 copy-done.2
  43.5 2.0 fusion.120
  45.5 1.9 copy.23
  47.4 1.7 fusion.4
  49.2 3.1 %slice.167 = f32[1536,128]{0,1:T(8,128)S(1)} slice(f32[1536,256]{0,1:T(8,128)} %fusion.4), slice={[0:1536:1], [1:256:2]} | slice | bytes 1572864 | tf_op jit(solution)/shard_map/slice | solution.py:223
  52.3 3.1 %slice.166 = f32[1536,128]{0,1:T(8,128)S(1)} slice(f32[1536,256]{0,1:T(8,128)} %fusion.4), slice={[0:1536:1], [0:256:2]} | slice | bytes 1572864 | tf_op jit(solution)/shard_map/slice | solution.py:223
  56.5 12.8 %collective-permute-start.3 = (bf16[768,128]{0,1:T(8,128)(2,1)S(1)}, bf16[768,128]{0,1:T(8,128)(2,1)S(1)}, u32[]{:S(2)}, u32[]{:S(2)}) collective-permute-start(bf16[768,128]{0,1:T(8,128)(2,1)S(1)} %rev.13), channel_id=1, source_target_pairs={{0,31},{1,30},{2,29},{3,28},{4,27},{5,26},{6,25},{7,24},{8,23},{9,... | collective-permute-start | bytes 589832 | tf_op jit(solution)/shard_map/ppermute | solution.py:192
  69.3 3.2 %collective-permute-done.3 = bf16[768,128]{0,1:T(8,128)(2,1)S(1)} collective-permute-done((bf16[768,128]{0,1:T(8,128)(2,1)S(1)}, bf16[768,128]{0,1:T(8,128)(2,1)S(1)}, u32[]{:S(2)}, u32[]{:S(2)}) %collective-permute-start.3) | collective-permute-done | bytes 196640 | tf_op jit(solution)/shard_map/ppermute | solution.py:192
  73.1 6.3 %collective-permute-start.4 = (bf16[1536,2]{0,1:T(2,128)(2,1)}, bf16[1536,2]{0,1:T(2,128)(2,1)}, u32[]{:S(2)}, u32[]{:S(2)}) collective-permute-start(bf16[1536,2]{0,1:T(2,128)(2,1)} %get-tuple-element.36), channel_id=1, source_target_pairs={{0,1},{1,2},{2,3},{3,4},{4,5},{5,6},{6,7},{7,8},{8,9},{9,10},{10,1... | collective-permute-start | bytes 18440 | tf_op jit(solution)/shard_map/ppermute | solution.py:183
  79.4 1.5 collective-permute-start.5
  81.2 1.4 mul.362
  82.7 1.6 mul.417
  84.3 5.8 %reshape.209 = bf16[12,128,5,128]{3,2,1,0:T(8,128)(2,1)} reshape(bf16[1,1,1536,640]{3,2,1,0:T(8,128)(2,1)} %get-tuple-element.21) | data formatting | bytes 3932160 | tf_op jit(solution)/shard_map/reshape;squeeze | solution.py:244
  90.0 2.4 copy.54
  92.4 3.5 %reshape.208 = bf16[12,128,5,128]{3,2,1,0:T(8,128)(2,1)} reshape(bf16[1,1,1536,640]{3,2,1,0:T(8,128)(2,1)S(1)} %copy-done.1) | data formatting | bytes 3932160 | tf_op jit(solution)/shard_map/reshape;squeeze | solution.py:244
  95.9 1.6 pad_maximum_fusion.5
  97.5 2.2 copy.24
  99.7 1.1 slice_dynamic-update-slice_fusion.9
  100.8 1.4 slice_dynamic-update-slice_fusion.8
  103.0 1.6 fusion.121
  104.6 1.5 copy.29
  106.1 1.5 fusion.59
  107.6 2.8 slice.180
  110.4 2.7 slice.179
  113.1 4.0 %collective-permute-start.6 = (bf16[1536,2]{0,1:T(2,128)(2,1)S(1)}, bf16[1536,2]{0,1:T(2,128)(2,1)S(1)}, u32[]{:S(2)}, u32[]{:S(2)}) collective-permute-start(bf16[1536,2]{0,1:T(2,128)(2,1)S(1)} %get-tuple-element.34), channel_id=1, source_target_pairs={{0,1},{1,2},{2,3},{3,4},{4,5},{5,6},{6,7},{7,8},{8,9},{9,10},{10,1... | collective-permute-start | bytes 18440 | tf_op jit(solution)/shard_map/ppermute | solution.py:183
  117.1 1.3 collective-permute-start.7
  118.4 1.8 fusion.101
  120.3 3.5 %convolution_convert_fusion.1 = bf16[12,128,640]{2,1,0:T(8,128)(2,1)} fusion(bf16[12,640,128]{2,1,0:T(8,128)(2,1)S(1)} %copy-done.6, f32[12,128,128]{1,2,0:T(8,128)} %fusion.121, f32[12,128,128]{2,1,0:T(8,128)} %copy.54), kind=kOutput, calls=%fused_computation.18 | convolution fusion | flops 256573440 | bytes 5505024 | tf_op jit(solution)/shard_map/gop,gkp->gok/dot_general | solution.py:237
  125.2 0.8 copy-done.14
  126.0 0.8 fusion.46
  127.3 10.5 %collective-permute-start.8 = (bf16[768,128]{0,1:T(8,128)(2,1)S(1)}, bf16[768,128]{0,1:T(8,128)(2,1)S(1)}, u32[]{:S(2)}, u32[]{:S(2)}) collective-permute-start(bf16[768,128]{0,1:T(8,128)(2,1)S(1)} %rev.14), channel_id=1, source_target_pairs={{0,31},{1,30},{2,29},{3,28},{4,27},{5,26},{6,25},{7,24},{8,23},{9,... | collective-permute-start | bytes 589832 | tf_op jit(solution)/shard_map/ppermute | solution.py:192
  138.0 2.9 collective-permute-done.8
  140.9 1.0 fusion.73
  142.8 2.2 mul.380
  145.0 2.6 mul.402
  147.7 2.9 fusion.25
  150.6 0.9 copy-done.13
  151.5 2.3 collective-permute-start.9
  153.8 1.3 collective-permute-start.10
  155.1 2.8 copy.52
  157.9 4.6 %convolution_convert_fusion = bf16[12,128,640]{2,1,0:T(8,128)(2,1)S(1)} fusion(bf16[12,640,256]{2,1,0:T(8,128)(2,1)} %copy-done.12, f32[12,256,128]{1,2,0:T(8,128)} %fusion.120, f32[12,128,256]{2,1,0:T(8,128)} %copy.52), kind=kOutput, calls=%fused_computation.17 | convolution fusion | flops 512163840 | bytes 9043968 | tf_op jit(solution)/shard_map/gop,gkp->gok/dot_general | solution.py:237
  162.5 2.3 pad_maximum_fusion.w
  164.8 2.3 mul.401
  167.1 1.3 pad_maximum_fusion.3
  168.4 0.7 copy.42
  170.5 1.2 copy-done.7
  171.7 0.9 fusion.37
  173.3 11.5 %collective-permute-start.11 = (bf16[768,256]{0,1:T(8,128)(2,1)S(1)}, bf16[768,256]{0,1:T(8,128)(2,1)S(1)}, u32[]{:S(2)}, u32[]{:S(2)}) collective-permute-start(bf16[768,256]{0,1:T(8,128)(2,1)S(1)} %rev.15), channel_id=1, source_target_pairs={{0,31},{1,30},{2,29},{3,28},{4,27},{5,26},{6,25},{7,24},{8,23},{9,... | collective-permute-start | bytes 1179656 | tf_op jit(solution)/shard_map/ppermute | solution.py:192
  185.2 1.0 fusion.117
  186.1 3.9 %collective-permute-done.11 = bf16[768,256]{0,1:T(8,128)(2,1)S(1)} collective-permute-done((bf16[768,256]{0,1:T(8,128)(2,1)S(1)}, bf16[768,256]{0,1:T(8,128)(2,1)S(1)}, u32[]{:S(2)}, u32[]{:S(2)}) %collective-permute-start.11) | collective-permute-done | bytes 393248 | tf_op jit(solution)/shard_map/ppermute | solution.py:192
  190.7 0.8 copy-done.11
  191.5 2.5 fusion.18
  193.9 2.3 copy.56
  196.2 2.1 copy-done
  198.3 98.3 %reduce_gradients.1 = (f32[2,48,640]{2,1,0:T(8,128)S(1)}, f32[32,128]{1,0:T(8,128)S(1)}) custom-call(bf16[2,2,4,4,48,640]{5,4,3,2,1,0:T(8,128)(2,1)S(1)} %copy-done, f32[32,128]{1,0:T(8,128)S(1)} %concatenate.61.dg), custom_call_target="tpu_custom_call" | custom-call | tf_op jit(solution)/shard_map/reduce_gradients/pallas_call | solution.py:154
  297.3 0.7 copy.94
  (109 shorter events, 12.4 us)
Async XLA Ops:
  3.1 0.6 copy-start.16
  4.2 28.5 %collective-permute-start = (bf16[768,256]{0,1:T(8,128)(2,1)S(1)}, bf16[768,256]{0,1:T(8,128)(2,1)S(1)}, u32[]{:S(2)}, u32[]{:S(2)}) collective-permute-start(bf16[768,256]{0,1:T(8,128)(2,1)S(1)} %rev.12), channel_id=1, source_target_pairs={{0,31},{1,30},{2,29},{3,28},{4,27},{5,26},{6,25},{7,24},{8,23},{9,... | collective-permute-start | bytes 1179656 | tf_op jit(solution)/shard_map/ppermute | solution.py:192
  32.8 7.5 %collective-permute-start.1 = (bf16[1536,2]{0,1:T(2,128)(2,1)S(1)}, bf16[1536,2]{0,1:T(2,128)(2,1)S(1)}, u32[]{:S(2)}, u32[]{:S(2)}) collective-permute-start(bf16[1536,2]{0,1:T(2,128)(2,1)S(1)} %get-tuple-element.28), channel_id=1, source_target_pairs={{0,1},{1,2},{2,3},{3,4},{4,5},{5,6},{6,7},{7,8},{8,9},{9,10},{10,1... | collective-permute-start | bytes 18440 | tf_op jit(solution)/shard_map/ppermute | solution.py:183
  34.6 5.8 %collective-permute-start.2 = (bf16[1536,2]{0,1:T(2,128)(2,1)S(1)}, bf16[1536,2]{0,1:T(2,128)(2,1)S(1)}, u32[]{:S(2)}, u32[]{:S(2)}) collective-permute-start(bf16[1536,2]{0,1:T(2,128)(2,1)S(1)} %get-tuple-element.29), channel_id=1, source_target_pairs={{1,0},{2,1},{3,2},{4,3},{5,4},{6,5},{7,6},{8,7},{9,8},{10,9},{11,1... | collective-permute-start | bytes 18440 | tf_op jit(solution)/shard_map/ppermute | solution.py:184
  42.0 1.5 copy-start.2
  42.6 2.9 copy-start.12
  47.4 1.8 copy-start.3
  55.6 25.2 %copy-start.15 = (bf16[1,1536,64]{1,2,0:T(8,128)(2,1)S(1)}, bf16[1,1536,64]{1,2,0:T(8,128)(2,1)}, u32[]{:S(2)}) copy-start(bf16[1,1536,64]{1,2,0:T(8,128)(2,1)} %param.5) | copy-start | bytes 589828
  55.7 0.5 copy-start.19
  56.5 15.9 %collective-permute-start.3 = (bf16[768,128]{0,1:T(8,128)(2,1)S(1)}, bf16[768,128]{0,1:T(8,128)(2,1)S(1)}, u32[]{:S(2)}, u32[]{:S(2)}) collective-permute-start(bf16[768,128]{0,1:T(8,128)(2,1)S(1)} %rev.13), channel_id=1, source_target_pairs={{0,31},{1,30},{2,29},{3,28},{4,27},{5,26},{6,25},{7,24},{8,23},{9,... | collective-permute-start | bytes 589832 | tf_op jit(solution)/shard_map/ppermute | solution.py:192
  73.1 22.8 %collective-permute-start.4 = (bf16[1536,2]{0,1:T(2,128)(2,1)}, bf16[1536,2]{0,1:T(2,128)(2,1)}, u32[]{:S(2)}, u32[]{:S(2)}) collective-permute-start(bf16[1536,2]{0,1:T(2,128)(2,1)} %get-tuple-element.36), channel_id=1, source_target_pairs={{0,1},{1,2},{2,3},{3,4},{4,5},{5,6},{6,7},{7,8},{8,9},{9,10},{10,1... | collective-permute-start | bytes 18440 | tf_op jit(solution)/shard_map/ppermute | solution.py:183
  79.4 16.5 %collective-permute-start.5 = (bf16[1536,2]{0,1:T(2,128)(2,1)}, bf16[1536,2]{0,1:T(2,128)(2,1)}, u32[]{:S(2)}, u32[]{:S(2)}) collective-permute-start(bf16[1536,2]{0,1:T(2,128)(2,1)} %get-tuple-element.37), channel_id=1, source_target_pairs={{1,0},{2,1},{3,2},{4,3},{5,4},{6,5},{7,6},{8,7},{9,8},{10,9},{11,1... | collective-permute-start | bytes 18440 | tf_op jit(solution)/shard_map/ppermute | solution.py:184
  84.3 8.2 %copy-start.1 = (bf16[1,1,1536,640]{3,2,1,0:T(8,128)(2,1)S(1)}, bf16[1,1,1536,640]{3,2,1,0:T(8,128)(2,1)}, u32[]{:S(2)}) copy-start(bf16[1,1,1536,640]{3,2,1,0:T(8,128)(2,1)} %get-tuple-element.20) | copy-start | bytes 5898244
  99.7 2.5 copy-start.4
  103.0 1.6 copy-start.5
  104.6 1.5 copy-start.9
  107.6 12.7 %copy-start.6 = (bf16[12,640,128]{2,1,0:T(8,128)(2,1)S(1)}, bf16[12,640,128]{2,1,0:T(8,128)(2,1)}, u32[]{:S(2)}) copy-start(bf16[12,640,128]{2,1,0:T(8,128)(2,1)} %copy-done.5) | copy-start | bytes 5898244
  113.1 10.6 %collective-permute-start.6 = (bf16[1536,2]{0,1:T(2,128)(2,1)S(1)}, bf16[1536,2]{0,1:T(2,128)(2,1)S(1)}, u32[]{:S(2)}, u32[]{:S(2)}) collective-permute-start(bf16[1536,2]{0,1:T(2,128)(2,1)S(1)} %get-tuple-element.34), channel_id=1, source_target_pairs={{0,1},{1,2},{2,3},{3,4},{4,5},{5,6},{6,7},{7,8},{8,9},{9,10},{10,1... | collective-permute-start | bytes 18440 | tf_op jit(solution)/shard_map/ppermute | solution.py:183
  117.1 6.6 %collective-permute-start.7 = (bf16[1536,2]{0,1:T(2,128)(2,1)S(1)}, bf16[1536,2]{0,1:T(2,128)(2,1)S(1)}, u32[]{:S(2)}, u32[]{:S(2)}) collective-permute-start(bf16[1536,2]{0,1:T(2,128)(2,1)S(1)} %get-tuple-element.35), channel_id=1, source_target_pairs={{1,0},{2,1},{3,2},{4,3},{5,4},{6,5},{7,6},{8,7},{9,8},{10,9},{11,1... | collective-permute-start | bytes 18440 | tf_op jit(solution)/shard_map/ppermute | solution.py:184
  124.1 1.9 copy-start.14
  127.3 13.6 %collective-permute-start.8 = (bf16[768,128]{0,1:T(8,128)(2,1)S(1)}, bf16[768,128]{0,1:T(8,128)(2,1)S(1)}, u32[]{:S(2)}, u32[]{:S(2)}) collective-permute-start(bf16[768,128]{0,1:T(8,128)(2,1)S(1)} %rev.14), channel_id=1, source_target_pairs={{0,31},{1,30},{2,29},{3,28},{4,27},{5,26},{6,25},{7,24},{8,23},{9,... | collective-permute-start | bytes 589832 | tf_op jit(solution)/shard_map/ppermute | solution.py:192
  137.8 4.1 %copy-start.10 = (f32[1536,128]{0,1:T(8,128)S(1)}, f32[1536,128]{0,1:T(8,128)}, u32[]{:S(2)}) copy-start(f32[1536,128]{0,1:T(8,128)} %mul.362) | copy-start | bytes 2359300
  138.0 4.0 %copy-start.20 = (f32[128]{0:T(128)S(1)}, f32[128]{0:T(128)}, u32[]{:S(2)}) copy-start(f32[128]{0:T(128)} %copy-done.19) | copy-start | bytes 1540
  150.6 0.9 copy-start.13
  151.5 15.6 %collective-permute-start.9 = (bf16[1536,2]{0,1:T(2,128)(2,1)S(1)}, bf16[1536,2]{0,1:T(2,128)(2,1)S(1)}, u32[]{:S(2)}, u32[]{:S(2)}) collective-permute-start(bf16[1536,2]{0,1:T(2,128)(2,1)S(1)} %get-tuple-element.24), channel_id=1, source_target_pairs={{0,1},{1,2},{2,3},{3,4},{4,5},{5,6},{6,7},{7,8},{8,9},{9,10},{10,1... | collective-permute-start | bytes 18440 | tf_op jit(solution)/shard_map/ppermute | solution.py:183
  153.8 13.3 %collective-permute-start.10 = (bf16[1536,2]{0,1:T(2,128)(2,1)S(1)}, bf16[1536,2]{0,1:T(2,128)(2,1)S(1)}, u32[]{:S(2)}, u32[]{:S(2)}) collective-permute-start(bf16[1536,2]{0,1:T(2,128)(2,1)S(1)} %get-tuple-element.25), channel_id=1, source_target_pairs={{1,0},{2,1},{3,2},{4,3},{5,4},{6,5},{7,6},{8,7},{9,8},{10,9},{11,1... | collective-permute-start | bytes 18440 | tf_op jit(solution)/shard_map/ppermute | solution.py:184
  157.9 4.6 %copy-start.8 = (bf16[12,128,640]{2,1,0:T(8,128)(2,1)S(1)}, bf16[12,128,640]{2,1,0:T(8,128)(2,1)}, u32[]{:S(2)}) copy-start(bf16[12,128,640]{2,1,0:T(8,128)(2,1)} %convolution_convert_fusion.1) | copy-start | bytes 5898244
  169.8 1.9 copy-start.7
  173.3 16.7 %collective-permute-start.11 = (bf16[768,256]{0,1:T(8,128)(2,1)S(1)}, bf16[768,256]{0,1:T(8,128)(2,1)S(1)}, u32[]{:S(2)}, u32[]{:S(2)}) collective-permute-start(bf16[768,256]{0,1:T(8,128)(2,1)S(1)} %rev.15), channel_id=1, source_target_pairs={{0,31},{1,30},{2,29},{3,28},{4,27},{5,26},{6,25},{7,24},{8,23},{9,... | collective-permute-start | bytes 1179656 | tf_op jit(solution)/shard_map/ppermute | solution.py:192
  185.1 4.9 %copy-start.17 = (f32[256]{0:T(256)S(1)}, f32[256]{0:T(256)}, u32[]{:S(2)}) copy-start(f32[256]{0:T(256)} %copy-done.16) | copy-start | bytes 3076
  190.1 1.4 copy-start.11
  190.1 1.4 copy-start.18
  196.2 2.1 copy-start

commit v2 on v1

v2 whole, which is shorter than its diff:
```python
import jax
import jax.numpy as jnp
from jax import lax
from jax.experimental import pallas as pl
from jax.experimental.pallas import tpu as pltpu
from jax.sharding import PartitionSpec as P

MESH = pl.DeviceIdType.MESH
F32 = jnp.float32
BF16 = jnp.bfloat16
COUNT = 15753216.0
CHANNELS = 1536.0
NT = (((1,), (1,)), ((), ()))
TN = (((0,), (0,)), ((), ()))


def iota(shape, dim):
    return lax.broadcasted_iota(jnp.int32, shape, dim)


def dot(a, b, dims=(((1,), (0,)), ((), ()))):
    return lax.dot_general(a, b, dims, preferred_element_type=F32)


def split_dot(a, b):
    high = a.astype(BF16)
    low = (a - high.astype(F32)).astype(BF16)
    return dot(high, b) + dot(low, b)


def reversal(length):
    shape = (length, length)
    return (iota(shape, 0) + iota(shape, 1) == length - 1).astype(F32).astype(BF16)


def pooling(length):
    shape = (length, length // 2)
    return jnp.where(iota(shape, 0) // 2 == iota(shape, 1), 0.5, 0.0).astype(BF16)


def spreading(length):
    shape = (length // 2, length)
    return jnp.where(iota(shape, 0) == iota(shape, 1) // 2, 0.5, 0.0).astype(BF16)


def edge_pick(slot, length):
    shape = (32, length)
    row = iota(shape, 0)
    j = row % 16 - 2 * slot
    target = j + jnp.where(row >= 16, length - 2, 0)
    hit = jnp.logical_and(jnp.logical_and(j >= 0, j < 2), iota(shape, 1) == target)
    return jnp.where(hit, 1.0, 0.0).astype(BF16)


def halo_place(slot, rows):
    shape = (rows, 128)
    row = iota(shape, 0)
    block = row // 16
    j = row % 16 - 2 * slot
    straight = jnp.where(block == 0, j, 126 + j)
    turned = jnp.where(block == 2, 1 - j, 127 - j)
    target = jnp.where(block < 2, straight, turned)
    hit = jnp.logical_and(jnp.logical_and(j >= 0, j < 2), iota(shape, 1) == target)
    return jnp.where(hit, 1.0, 0.0).astype(BF16)


def as_row(column):
    shape = (128, 128)
    return jnp.sum(jnp.where(iota(shape, 0) == iota(shape, 1), column, 0.0), axis=0, keepdims=True)


def fold(value):
    rows, length = value.shape
    return jnp.sum(value.reshape(rows // 8, 8, length), axis=0)


def gelu_parts(y):
    c0 = 0.7978845608028654
    square = y * y
    t = jnp.tanh(c0 * (y + 0.044715 * (square * y)))
    cdf = 0.5 * (1.0 + t)
    slope = cdf + 0.5 * y * (1.0 - t * t) * (c0 * (1.0 + 0.134145 * square))
    return y * cdf, slope


def kernel(h0, cot, wt_in, gain, sec_out, ig_out, out, gout,
           gcol, wtr, nb0, nb1, h1, s0, s1, gp0, dr0, dr1, dyb0, dyb1, dn0, dn1, dzs0, dzs1, nrev,
           rc0, rc1, rc2, rc3, esend, eright, eleft, eright_m, eleft_m, dgb,
           w, ra, rb, pa, pb, qa, qb, sab, tz, gbuf, g1, g2, g3, sq, sq1, sq2,
           psend, precv, esem, ersem,
           ss1, rs1, ss2, rs2, ss3, rs3, sg, rg, sn, rn):
    sec = lax.axis_index("section")
    me = lax.axis_index("ctx")
    z = me // 16
    x = (me // 4) % 4
    y = me % 4
    plane = me % 16
    line = sec * 2 + z
    has_left = me > 0
    has_right = me < 31
    not_15 = jnp.logical_and(has_right, me != 15)
    not_16 = jnp.logical_and(has_left, me != 16)

    def ctx(index):
        return {"section": sec, "ctx": index}

    def at_x(d):
        return ctx(z * 16 + ((x + d) % 4) * 4 + y)

    def at_y(d):
        return ctx(z * 16 + x * 4 + (y + d) % 4)

    def at_z():
        return ctx((1 - z) * 16 + plane)

    def at_plane(d):
        return ctx(z * 16 + (plane + d) % 16)

    def at_line(d):
        other = (line + d) % 16
        return {"section": other // 2, "ctx": (other % 2) * 16 + plane}

    to_mirror = ctx(31 - me)
    to_left = ctx((me + 31) % 32)
    to_right = ctx((me + 1) % 32)
    to_right_m = ctx((62 - me) % 32)
    to_left_m = ctx((32 - me) % 32)

    def copy(src, dst, send, recv, device):
        return pltpu.make_async_remote_copy(
            src_ref=src, dst_ref=dst, send_sem=send, recv_sem=recv,
            device_id=device, device_id_type=MESH)

    eright[...] = jnp.zeros_like(eright)
    eleft[...] = jnp.zeros_like(eleft)
    eright_m[...] = jnp.zeros_like(eright_m)
    eleft_m[...] = jnp.zeros_like(eleft_m)
    dgb[...] = jnp.zeros_like(dgb)

    barrier = pltpu.get_barrier_semaphore()

    def greet(device):
        pl.semaphore_signal(barrier, inc=1, device_id=device, device_id_type=MESH)

    greet(to_mirror)
    for d in range(1, 16):
        greet(at_plane(d))
        greet(at_line(d))

    @pl.when(has_left)
    def _():
        greet(to_left)

    @pl.when(has_right)
    def _():
        greet(to_right)

    @pl.when(not_15)
    def _():
        greet(to_right_m)

    @pl.when(not_16)
    def _():
        greet(to_left_m)

    def edge_copies(s):
        left = copy(esend.at[s, 0], eright.at[s], esem.at[s, 0], ersem.at[s, 0], to_left)
        right = copy(esend.at[s, 1], eleft.at[s], esem.at[s, 1], ersem.at[s, 1], to_right)
        right_m = left_m = None
        if s < 2:
            right_m = copy(esend.at[s, 1, 1], eright_m.at[s], esem.at[s, 2], ersem.at[s, 2], to_right_m)
            left_m = copy(esend.at[s, 0, 1], eleft_m.at[s], esem.at[s, 3], ersem.at[s, 3], to_left_m)
        return left, right, right_m, left_m

    def edges_start(s):
        left, right, right_m, left_m = edge_copies(s)
        pl.when(has_left)(left.start)
        pl.when(has_right)(right.start)
        if s < 2:
            pl.when(not_15)(right_m.start)
            pl.when(not_16)(left_m.start)

            @pl.when(me == 15)
            def _():
                eright_m[s] = esend[s, 1, 1]

            @pl.when(me == 16)
            def _():
                eleft_m[s] = esend[s, 0, 1]

    def edges_wait(s):
        left, right, right_m, left_m = edge_copies(s)
        pl.when(has_left)(left.wait_send)
        pl.when(has_right)(left.wait_recv)
        pl.when(has_right)(right.wait_send)
        pl.when(has_left)(right.wait_recv)
        if s < 2:
            pl.when(not_15)(right_m.wait)
            pl.when(not_16)(left_m.wait)

    def edges_store(s, half, value):
        esend[s, 0, half] = value[0:16].astype(BF16)
        esend[s, 1, half] = value[16:32].astype(BF16)

    def halo(s, half, slot, mirrored):
        parts = [eright[s, half], eleft[s, half]]
        if mirrored:
            parts += [eright_m[s], eleft_m[s]]
        return dot(jnp.concatenate(parts, axis=0), halo_place(slot, 16 * len(parts)), TN)

    def panel(step, g):
        src, dst = ((nb0.at[g + 6], rc0.at[g]), (nb1.at[g + 6], rc1.at[g]),
                    (dzs1.at[g], rc2.at[g]), (dzs0.at[g], rc3.at[g]))[step]
        return copy(src, dst, psend.at[step, g], precv.at[step, g], to_mirror)

    def shifted(value, tail, sign, store):
        length = value.shape[1]
        wide = jnp.concatenate([value, tail], axis=1)
        for k in range(5):
            shift = (sign * (2 - k)) % (length + 128)
            turned = wide if shift == 0 else pltpu.roll(wide, shift, 1)
            store(k, turned[:, :length].astype(BF16))

    @pl.loop(0, 24)
    def _(i):
        shape = (128, 128)
        column = jnp.sum(
            jnp.where(iota(shape, 0) == iota(shape, 1), gain[pl.ds(i, 1), :], 0.0), axis=1, keepdims=True)
        gcol[i] = jnp.broadcast_to(column, shape)

    def inverse_of(total):
        return lax.rsqrt(jnp.sum(total, axis=0, keepdims=True) / CHANNELS + 1e-06)

    def norm(block, acts, inverse, length, target, s):
        g_wide = length // 128
        for half in (1, 0):
            def body(i, edge):
                g = half * 6 + i
                column = gcol[block * 12 + g]
                wide = jnp.concatenate([column] * g_wide, axis=1)
                value = ((acts[g].astype(F32) * inverse) * wide).astype(BF16)
                target[g] = value
                return edge + dot(edge_pick(i, length), value, NT)
            edges_store(s, half, lax.fori_loop(0, 6, body, jnp.zeros((32, 128), F32)))

    total0 = lax.fori_loop(
        0, 12, lambda g, t: t + fold(jnp.square(h0[g].astype(F32))), jnp.zeros((8, 256), F32))
    inv0 = inverse_of(total0)
    norm(0, h0, inv0, 256, nb0, 0)

    pl.semaphore_wait(
        barrier, 31 + has_left.astype(jnp.int32) + has_right.astype(jnp.int32)
        + not_15.astype(jnp.int32) + not_16.astype(jnp.int32))
    edges_start(0)

    @pl.loop(0, 6)
    def _(g):
        panel(0, g).start()

    @pl.loop(0, 12)
    def _(g):
        for b in range(2):
            for k in range(5):
                wtr[b, g, :, k * 128:(k + 1) * 128] = wt_in[b, g, :, k * 128:(k + 1) * 128].T

    edges_wait(0)

    def conv0(g, value, tail):
        def store(k, part):
            s0[g, k * 128:(k + 1) * 128, :] = part
        shifted(value, tail, 1, store)
        act, slope = gelu_parts(dot(wt_in[0, g], s0[g]))
        gp0[g] = slope
        res = h0[g].astype(F32) + act
        pooled = split_dot(res, pooling(256)).astype(BF16)
        h1[g] = pooled
        return fold(jnp.square(pooled.astype(F32)))

    def hi0(i, t):
        g = i + 6
        return t + conv0(g, nb0[g].astype(F32), halo(0, 1, i, False))

    def lo0(g, t):
        panel(0, g).wait()
        turned = dot(rc0[g], reversal(256))
        nrev[g] = turned.astype(BF16)
        return t + conv0(g, nb0[g].astype(F32) + turned, halo(0, 0, g, True))

    total1 = lax.fori_loop(0, 6, hi0, jnp.zeros((8, 128), F32))
    total1 = lax.fori_loop(0, 6, lo0, total1)
    inv1 = inverse_of(total1)
    norm(1, h1, inv1, 128, nb1, 1)
    edges_start(1)

    @pl.loop(0, 6)
    def _(g):
        panel(1, g).start()

    edges_wait(1)

    def conv1(g, slot, value, tail):
        def store(k, part):
            s1[g, k * 128:(k + 1) * 128, :] = part
        shifted(value, tail, 1, store)
        act, slope = gelu_parts(dot(wt_in[1, g], s1[g]))
        res = h1[g].astype(F32) + act
        sec_out[g] = split_dot(res, pooling(128)).astype(BF16)
        dr = dot(cot[g], spreading(128))
        dr1[g] = dr
        dy = (dr * slope).astype(BF16)
        dyb1[g] = dy
        return dot(edge_pick(slot, 128), dy, NT)

    def hi1(i, e):
        g = i + 6
        return e + conv1(g, i, nb1[g].astype(F32), halo(1, 1, i, False))

    def lo1(g, e):
        panel(1, g).wait()
        turned = dot(rc1[g], reversal(128))
        return e + conv1(g, g, nb1[g].astype(F32) + turned, halo(1, 0, g, True))

    edges_store(2, 1, lax.fori_loop(0, 6, hi1, jnp.zeros((32, 128), F32)))
    edges_store(2, 0, lax.fori_loop(0, 6, lo1, jnp.zeros((32, 128), F32)))
    edges_start(2)

    def weight_grads(b, dyb, stacks):
        @pl.loop(0, 12)
        def _(i):
            g = (i + 6) % 12
            grad = dot(dyb[g], stacks[g], NT).astype(BF16)
            for j in range(8):
                piece = g * 8 + j
                block = piece // 3
                w[b, block // 16, (block // 4) % 4, block % 4, piece % 3] = grad[j * 16:(j + 1) * 16]

    def first(b):
        cps = []
        for d in range(1, 4):
            cps.append(copy(w.at[b, 1, :, (y + d) % 4], rb.at[b, d - 1],
                            ss1.at[b, 1, d - 1], rs1.at[b, 1, d - 1], at_y(d)))
            cps.append(copy(w.at[b, 0, (x + d) % 4], ra.at[b, d - 1],
                            ss1.at[b, 0, d - 1], rs1.at[b, 0, d - 1], at_x(d)))
        return cps

    def second(b):
        cps = []
        for d in range(1, 4):
            cps.append(copy(pa.at[b, (y + d) % 4], qa.at[b, d - 1],
                            ss2.at[b, 0, d - 1], rs2.at[b, 0, d - 1], at_y(d)))
            cps.append(copy(pb.at[b, (x + d) % 4], qb.at[b, d - 1],
                            ss2.at[b, 1, d - 1], rs2.at[b, 1, d - 1], at_x(d)))
        return cps

    def third(b):
        return copy(sab.at[b, 1 - z], tz.at[b], ss3.at[b], rs3.at[b], at_z())

    def add_first(b):
        for cp in first(b):
            cp.wait()

        @pl.loop(0, 4)
        def _(k):
            a = w[b, 0, x, k].astype(F32)
            c = w[b, 1, k, y].astype(F32)
            for d in range(3):
                a += ra[b, d, k].astype(F32)
                c += rb[b, d, k].astype(F32)
            pa[b, k] = a.astype(BF16)
            pb[b, k] = c.astype(BF16)
        for cp in second(b):
            cp.start()

    def add_second(b):
        for cp in second(b):
            cp.wait()
        a = pa[b, y].astype(F32)
        c = pb[b, x].astype(F32)
        for d in range(3):
            a += qa[b, d].astype(F32)
            c += qb[b, d].astype(F32)
        sab[b, 0] = a.astype(BF16)
        sab[b, 1] = c.astype(BF16)
        third(b).start()

    weight_grads(1, dyb1, s1)
    for cp in first(1):
        cp.start()
    edges_wait(2)

    def back(b, g, slot, half, s, dyb, length):
        parts = [None] * 5

        def store(k, part):
            parts[k] = part
        shifted(dyb[g].astype(F32), halo(s, half, slot, False), -1, store)
        return dot(wtr[b, g], jnp.concatenate(parts, axis=0)).astype(BF16)

    def scaled_sum(dn, xhat, row, length):
        weighted = dn * xhat
        column = jnp.sum(weighted, axis=1, keepdims=True)
        return fold(weighted * jnp.concatenate([gcol[row]] * (length // 128), axis=1)), as_row(column)

    def lo1_back(g, q):
        dz = back(1, g, g, 0, 2, dyb1, 128)
        dzs1[g] = dz
        panel(2, g).start()
        dn = dz.astype(F32)
        dn1[g] = dn
        part, row = scaled_sum(dn, h1[g].astype(F32) * inv1, 12 + g, 128)
        dgb[pl.ds(12 + g, 1), :] = row
        return q + part

    q1 = lax.fori_loop(0, 6, lo1_back, jnp.zeros((8, 128), F32))

    @pl.loop(6, 12)
    def _(g):
        dn1[g] = back(1, g, g - 6, 1, 2, dyb1, 128).astype(F32)

    def hi1_back(i, q):
        g = i + 6
        panel(2, i).wait()
        dn = dn1[g] + dot(rc2[i], reversal(128))
        dn1[g] = dn
        part, row = scaled_sum(dn, h1[g].astype(F32) * inv1, 12 + g, 128)
        dgb[pl.ds(12 + g, 1), :] = row
        return q + part

    q1 = lax.fori_loop(0, 6, hi1_back, q1)
    mean1 = jnp.sum(q1, axis=0, keepdims=True) / CHANNELS

    for half in (1, 0):
        def step(i, e):
            g = half * 6 + i
            xhat = h1[g].astype(F32) * inv1
            dh = (dn1[g] * gcol[12 + g] - xhat * mean1) * inv1 + dr1[g]
            dr = split_dot(dh, spreading(256))
            dr0[g] = dr
            dy = (dr * gp0[g]).astype(BF16)
            dyb0[g] = dy
            return e + dot(edge_pick(i, 256), dy, NT)
        edges_store(3, half, lax.fori_loop(0, 6, step, jnp.zeros((32, 128), F32)))
    edges_start(3)
    weight_grads(0, dyb0, s0)
    for cp in first(0):
        cp.start()
    add_first(1)
    edges_wait(3)

    def lo0_back(g, q):
        dz = back(0, g, g, 0, 3, dyb0, 256)
        dzs0[g] = dz
        panel(3, g).start()
        dn = dz.astype(F32)
        dn0[g] = dn
        part, row = scaled_sum(dn, h0[g].astype(F32) * inv0, g, 256)
        dgb[pl.ds(g, 1), :] = row
        column = jnp.sum(dn * nrev[g].astype(F32), axis=1, keepdims=True) / gcol[6 + g]
        dgb[pl.ds(6 + g, 1), :] = as_row(column)
        return q + part

    q0 = lax.fori_loop(0, 6, lo0_back, jnp.zeros((8, 256), F32))

    @pl.loop(6, 12)
    def _(g):
        dn = back(0, g, g - 6, 1, 3, dyb0, 256).astype(F32)
        dn0[g] = dn
        column = jnp.sum(dn * (h0[g].astype(F32) * inv0), axis=1, keepdims=True)
        dgb[pl.ds(g, 1), :] += as_row(column)

    gbuf[0] = dgb[...]
    gx = [copy(gbuf.at[0], g1.at[d - 1], sg.at[0, d - 1], rg.at[0, d - 1], at_x(d)) for d in range(1, 4)]
    gy = [copy(gbuf.at[1], g2.at[d - 1], sg.at[1, d - 1], rg.at[1, d - 1], at_y(d)) for d in range(1, 4)]
    gz = copy(gbuf.at[2], g3, sg.at[2, 0], rg.at[2, 0], at_z())
    for cp in gx:
        cp.start()
    add_second(1)
    add_first(0)
    for cp in gx:
        cp.wait()
    gbuf[1] = gbuf[0] + g1[0] + g1[1] + g1[2]
    for cp in gy:
        cp.start()
    add_second(0)
    for cp in gy:
        cp.wait()
    gbuf[2] = gbuf[1] + g2[0] + g2[1] + g2[2]
    gz.start()

    def hi0_back(i, q):
        g = i + 6
        panel(3, i).wait()
        dn = dn0[g] + dot(rc3[i], reversal(256))
        dn0[g] = dn
        xhat = h0[g].astype(F32) * inv0
        return q + fold(dn * xhat * jnp.concatenate([gcol[g]] * 2, axis=1))

    q0 = lax.fori_loop(0, 6, hi0_back, q0)
    mean0 = jnp.sum(q0, axis=0, keepdims=True) / CHANNELS

    gz.wait()
    total_g = gbuf[2] + g3[...]
    square = jnp.sum(total_g * total_g) * (1.0 / 32.0)
    for b in (1, 0):
        third(b).wait()
        full = sab[b, z].astype(F32) + tz[b].astype(F32)
        out[b] = full
        square += jnp.sum(full * full)
    sq[0] = jnp.full((8, 128), square, F32)
    near = [copy(sq.at[0], sq1.at[d - 1], sn.at[0, d - 1], rn.at[0, d - 1], at_plane(d)) for d in range(1, 16)]
    for cp in near:
        cp.start()

    @pl.loop(0, 12)
    def _(g):
        xhat = h0[g].astype(F32) * inv0
        wide = jnp.concatenate([gcol[g]] * 2, axis=1)
        ig_out[g] = ((dn0[g] * wide - xhat * mean0) * inv0 + dr0[g]).astype(BF16)

    for cp in near:
        cp.wait()
    sq[1] = sq[0] + jnp.sum(sq1[...], axis=0)
    far = [copy(sq.at[1], sq2.at[d - 1], sn.at[1, d - 1], rn.at[1, d - 1], at_line(d)) for d in range(1, 16)]
    for cp in far:
        cp.start()
    for cp in far:
        cp.wait()
    total = sq[1] + jnp.sum(sq2[...], axis=0)
    factor = jnp.minimum(1.0, lax.rsqrt(total / COUNT + 1e-06))[0:1, 0:1]
    for b in range(2):
        out[b] = out[b] * factor
    gout[...] = total_g * factor


def local(section_input, out_cotangent, conv_weight, norm_gain):
    h0 = section_input.reshape(12, 128, 256)
    cot = out_cotangent.reshape(12, 128, 64)
    weights = conv_weight.reshape(2, 12, 128, 640)
    gain = norm_gain.reshape(24, 128)
    dma = pltpu.SemaphoreType.DMA

    def vm(shape, kind=BF16):
        return pltpu.VMEM(shape, kind)

    second, grad_in, wshare, gfull = pl.pallas_call(
        kernel,
        out_shape=(
            jax.ShapeDtypeStruct((12, 128, 64), BF16),
            jax.ShapeDtypeStruct((12, 128, 256), BF16),
            jax.ShapeDtypeStruct((2, 3, 16, 640), F32),
            jax.ShapeDtypeStruct((32, 128), F32),
        ),
        in_specs=[pl.BlockSpec(memory_space=pltpu.VMEM)] * 4,
        out_specs=[pl.BlockSpec(memory_space=pltpu.VMEM)] * 4,
        scratch_shapes=[
            vm((24, 128, 128), F32), vm((2, 12, 128, 640)),
            vm((12, 128, 256)), vm((12, 128, 128)), vm((12, 128, 128)),
            vm((12, 640, 256)), vm((12, 640, 128)),
            vm((12, 128, 256), F32), vm((12, 128, 256), F32), vm((12, 128, 128), F32),
            vm((12, 128, 256)), vm((12, 128, 128)),
            vm((12, 128, 256), F32), vm((12, 128, 128), F32),
            vm((6, 128, 256)), vm((6, 128, 128)), vm((6, 128, 256)),
            vm((6, 128, 256)), vm((6, 128, 128)), vm((6, 128, 128)), vm((6, 128, 256)),
            vm((4, 2, 2, 16, 128)), vm((4, 2, 16, 128)), vm((4, 2, 16, 128)),
            vm((2, 16, 128)), vm((2, 16, 128)), vm((32, 128), F32),
            vm((2, 2, 4, 4, 3, 16, 640)), vm((2, 3, 4, 3, 16, 640)), vm((2, 3, 4, 3, 16, 640)),
            vm((2, 4, 3, 16, 640)), vm((2, 4, 3, 16, 640)),
            vm((2, 3, 3, 16, 640)), vm((2, 3, 3, 16, 640)),
            vm((2, 2, 3, 16, 640)), vm((2, 3, 16, 640)),
            vm((3, 32, 128), F32), vm((3, 32, 128), F32), vm((3, 32, 128), F32), vm((32, 128), F32),
            vm((2, 8, 128), F32), vm((15, 8, 128), F32), vm((15, 8, 128), F32),
            dma((4, 6)), dma((4, 6)), dma((4, 4)), dma((4, 4)),
            dma((2, 2, 3)), dma((2, 2, 3)), dma((2, 2, 3)), dma((2, 2, 3)), dma((2,)), dma((2,)),
            dma((3, 3)), dma((3, 3)), dma((2, 15)), dma((2, 15)),
        ],
        compiler_params=pltpu.CompilerParams(
            collective_id=0, has_side_effects=True, vmem_limit_bytes=56 << 20),
        name="tower",
    )(h0, cot, weights, gain)
    me = lax.axis_index("ctx")
    gshare = lax.dynamic_slice(gfull[:24].reshape(2, 1536), (0, me * 48), (2, 48))
    return (
        second.reshape(1, 1536, 64),
        grad_in.reshape(1, 1536, 256),
        wshare.reshape(1, 2, 48, 640),
        gshare[None],
    )


def solution(mesh):
    placed = (
        P("section", None, "ctx"),
        P("section", None, "ctx"),
        P("section", None, None, None),
        P("section", None, None),
    )
    return jax.shard_map(
        local,
        mesh=mesh,
        in_specs=placed,
        out_specs=(
            P("section", None, "ctx"),
            P("section", None, "ctx"),
            P("section", None, "ctx", None),
            P("section", None, "ctx"),
        ),
        check_vma=False,
    )
```

time: 299 us -> 137 us (0.46)
  starting transfers between devices: 67 us -> 0 us
  local copies, waits for them, and re-layouts: 71.4 us -> 10.1 us
  Pallas kernels: 98.3 us -> 126 us
  waiting for transfers between devices: 26 us -> 0 us
  other arithmetic: 20.7 us -> 0 us
  matrix products: 13.3 us -> 0 us
    ppermute x12 -> x0, starting transfers between devices: 67 us -> none  [the longest x4 47.2 us: mirror(): return lax.ppermute(panel[:, ::-1], 'ctx', pairs)]
    pallas_call x1, Pallas kernels: 98.3 us -> 126 us  [local(): pl.pallas_call(kernel, out_shape=(jax.ShapeDtypeStruct((12, 128, 64), BF1...]
    ppermute x12 -> x0, waiting for transfers between devices: 26 us -> none  [the longest x4 26 us: mirror(): return lax.ppermute(panel[:, ::-1], 'ctx', pairs)]
    slice x14 -> x0, local copies, waits for them, and re-layouts: 17.6 us -> none  [the longest x4 11.8 us: forward_block(): output = (0.5 * (resid[:, 0::2] + resid[:, 1::2])).astype(jnp.bfloat16)]
    mul x7 -> x0, local copies, waits for them, and re-layouts: 15.4 us -> none  [backward_block(): grad_res = jnp.repeat(grad_out, 2, axis=1) * 0.5]
    dot_general x6 -> x0, matrix products: 13.3 us -> none  [the longest x2 8.03 us: backward_block(): jnp.einsum('gop,gkp->gok', pre_group, stacked, preferred_element_type=jnp...]
    unnamed x61 -> x4, local copies, waits for them, and re-layouts: 17.9 us -> 7.39 us
    another operation x6 -> x0, local copies, waits for them, and re-layouts: 9.4 us -> none  [the longest x2 9.24 us: backward_block(): wfour = weight.reshape(groups, width, 5, width)]
  transfers between devices with their start and end apart: 12 -> 0, of which waited for: 4 -> 0; matrix products, arithmetic and copies ran while one was open for 13% -> 0% of each run, Pallas kernels for 0% -> 0%
where the time goes in v2:
time: 137 us
  Pallas kernels  126 us (92%)
  local copies, waits for them, and re-layouts  10.1 us (7%)
    pallas_call x1, Pallas kernels, local(): pl.pallas_call(kernel, out_shape=(jax.ShapeDtypeStruct((12, 128, 64), BF1...  126 us
    unnamed x4, local copies, waits for them, and re-layouts  7.39 us

profile of v2, /device:TPU:1, one launch (start us, length us, event | category | flops | bytes accessed | tf_op | source)
XLA Modules:
  0.0 136.8 jit_solution(15628447053776112592)
XLA Ops:
  0.6 1.8 %copy.8 = bf16[1,1536,64]{2,1,0:T(8,128)(2,1)} copy(bf16[1,1536,64]{1,2,0:T(8,128)(2,1)} %param.5) | data formatting | bytes 393216 | tf_op args[1]
  2.5 1.3 reshape.35.gain
  3.8 126.1 %tower.1 = (bf16[12,128,64]{2,1,0:T(8,128)(2,1)}, bf16[12,128,256]{2,1,0:T(8,128)(2,1)}, f32[2,3,16,640]{3,2,1,0:T(8,128)}, f32[32,128]{1,0:T(8,128)}) custom-call(bf16[12,128,256]{2,1,0:T(8,128)(2,1)} %bitcast.11, bf16[12,128,64]{2,1,0:T(8,128)(2,1)} %bitcast.9, bf16[2,12,128,640]{3,2,1,0:T(8,128)(2,1)} %bitcast.8, f32[24,128]{1,0:T(8,128)} %reshape.35.gain), custom_call_target="tpu_custom_call" | custom-call | tf_op jit(solution)/shard_map/tower/pallas_call | solution.py:545
  129.9 1.8 %copy.9 = bf16[1,1536,64]{1,2,0:T(8,128)(2,1)} copy(bf16[1,1536,64]{2,1,0:T(8,128)(2,1)} %bitcast.12) | data formatting | bytes 393216
  131.7 0.7 slice.3
  132.5 0.6 dynamic-slice_bitcast_fusion
  133.1 2.1 %copy.12 = bf16[1,1536,256]{2,1,0:T(8,128)(2,1)} copy(bf16[1,1536,256]{2,1,0:T(8,128)(2,1)} %bitcast.10) | data formatting | bytes 1572864
  135.2 1.7 %copy.13 = f32[1,2,48,640]{3,2,1,0:T(8,128)} copy(f32[1,2,48,640]{3,2,1,0:T(8,128)} %bitcast.13) | data formatting | bytes 491520
  (1 shorter events, 0.0 us)

commit v3 on v2

v3 whole, which is shorter than its diff:
```python
import jax
import jax.numpy as jnp
from jax import lax
from jax.experimental import pallas as pl
from jax.experimental.pallas import tpu as pltpu
from jax.sharding import PartitionSpec as P

MESH = pl.DeviceIdType.MESH
F32 = jnp.float32
BF16 = jnp.bfloat16
COUNT = 15753216.0
CHANNELS = 1536.0
PER = 6
NT = (((1,), (1,)), ((), ()))
TN = (((0,), (0,)), ((), ()))


def iota(shape, dim):
    return lax.broadcasted_iota(jnp.int32, shape, dim)


def dot(a, b, dims=(((1,), (0,)), ((), ()))):
    return lax.dot_general(a, b, dims, preferred_element_type=F32)


def two_terms(a):
    high = a.astype(BF16)
    return high, (a - high.astype(F32)).astype(BF16)


def reversal(length):
    shape = (length, length)
    return jnp.where(iota(shape, 0) + iota(shape, 1) == length - 1, 1.0, 0.0).astype(BF16)


def spreading(length):
    shape = (length // 2, length)
    return jnp.where(iota(shape, 0) == iota(shape, 1) // 2, 0.5, 0.0).astype(BF16)


def edge_pick(slot, length):
    shape = (32, length)
    row = iota(shape, 0)
    j = row % 16 - 2 * slot
    target = j + jnp.where(row >= 16, length - 2, 0)
    hit = jnp.logical_and(jnp.logical_and(j >= 0, j < 2), iota(shape, 1) == target)
    return jnp.where(hit, 1.0, 0.0).astype(BF16)


def halo_place(slot):
    shape = (64, 128)
    row = iota(shape, 0)
    block = row // 16
    j = row % 16 - 2 * slot
    straight = jnp.where(block == 0, j, 126 + j)
    turned = jnp.where(block == 2, 1 - j, 127 - j)
    target = jnp.where(block < 2, straight, turned)
    hit = jnp.logical_and(jnp.logical_and(j >= 0, j < 2), iota(shape, 1) == target)
    return jnp.where(hit, 1.0, 0.0).astype(BF16)


def wide(column, length):
    return column if length == 128 else jnp.concatenate([column] * (length // 128), axis=1)


def run(low, high, body, carry, per):
    if per >= high - low:
        for i in range(low, high):
            carry = body(i, carry)
        return carry

    def several(k, c):
        for u in range(per):
            c = body(low + k * per + u, c)
        return c
    return lax.fori_loop(0, (high - low) // per, several, carry)


def as_row(column):
    shape = (128, 128)
    return jnp.sum(jnp.where(iota(shape, 0) == iota(shape, 1), column, 0.0), axis=0, keepdims=True)


def fold(value):
    rows, length = value.shape
    return jnp.sum(value.reshape(rows // 8, 8, length), axis=0)


def gelu_parts(y):
    c0 = 0.7978845608028654
    square = y * y
    t = jnp.tanh(c0 * (y + 0.044715 * (square * y)))
    cdf = 0.5 * (1.0 + t)
    slope = cdf + 0.5 * y * (1.0 - t * t) * (c0 * (1.0 + 0.134145 * square))
    return y * cdf, slope


def kernel(h0_hbm, cot, wt_hbm, gain, sec_hbm, ig_hbm, out, gout,
           h0, wt_in, secb, igb, rev, spread, pick0, pick1, place, iv0s, iv1s, iv0r, iv1r, gfull,
           gcol, wtr, nb0, nb1, h1, s0, s1, gp0, dr0, dr1, dyb0, dyb1, dn0, dn1, dzs0, dzs1, nrev,
           rc0, rc1, rc2, rc3, esend, eright, eleft, eright_m, eleft_m, dgb,
           w, rr, pp, qq, sab, tz, nrev1, qs, qr, gbuf, g1, g2, g3, sq, sq1, sq2,
           psend, precv, esem, ersem, ivsem, ivrsem, lsem, qsem, qrsem,
           ss1, rs1, ss2, rs2, ss3, rs3, sg, rg, sn, rn):
    sec = lax.axis_index("section")
    me = lax.axis_index("ctx")
    z = me // 16
    x = (me // 4) % 4
    y = me % 4
    plane = me % 16
    line = sec * 2 + z
    has_left = me > 0
    has_right = me < 31
    not_15 = jnp.logical_and(has_right, me != 15)
    not_16 = jnp.logical_and(has_left, me != 16)

    def ctx(index):
        return {"section": sec, "ctx": index}

    def at_x(d):
        return ctx(z * 16 + ((x + d) % 4) * 4 + y)

    def at_y(d):
        return ctx(z * 16 + x * 4 + (y + d) % 4)

    def at_z():
        return ctx((1 - z) * 16 + plane)

    def at_plane(d):
        return ctx(z * 16 + (plane + d) % 16)

    def at_line(d):
        other = (line + d) % 16
        return {"section": other // 2, "ctx": (other % 2) * 16 + plane}

    to_mirror = ctx(31 - me)
    to_left = ctx((me + 31) % 32)
    to_right = ctx((me + 1) % 32)
    to_right_m = ctx((62 - me) % 32)
    to_left_m = ctx((32 - me) % 32)

    def copy(src, dst, send, recv, device):
        return pltpu.make_async_remote_copy(
            src_ref=src, dst_ref=dst, send_sem=send, recv_sem=recv,
            device_id=device, device_id_type=MESH)

    eright[...] = jnp.zeros_like(eright)
    eleft[...] = jnp.zeros_like(eleft)
    eright_m[...] = jnp.zeros_like(eright_m)
    eleft_m[...] = jnp.zeros_like(eleft_m)
    dgb[...] = jnp.zeros_like(dgb)

    barrier = pltpu.get_barrier_semaphore()

    def greet(device):
        pl.semaphore_signal(barrier, inc=1, device_id=device, device_id_type=MESH)

    greet(to_mirror)

    @pl.when(not_15)
    def _():
        greet(to_right_m)

    @pl.when(not_16)
    def _():
        greet(to_left_m)

    for d in (8, 7, 9, 6, 10, 5, 11, 4, 12, 3, 13, 2, 14, 1, 15):
        greet(at_line(d))

    @pl.when(has_left)
    def _():
        greet(to_left)

    @pl.when(has_right)
    def _():
        greet(to_right)

    for d in range(1, 16):
        greet(at_plane(d))

    h0_load = pltpu.make_async_copy(h0_hbm, h0, lsem.at[0])
    w_load = pltpu.make_async_copy(wt_hbm, wt_in, lsem.at[1])
    h0_load.start()
    w_load.start()

    for b in range(2):
        value = jnp.broadcast_to(gain[b:b + 1, :], (16, 1536))
        top = value.astype(BF16).astype(F32)
        middle = (value - top).astype(BF16).astype(F32)
        rest = value - top - middle
        row = iota((16, 1536), 0)
        terms = jnp.where(row == 0, top, jnp.where(row == 1, middle, jnp.where(row == 2, rest, 0.0)))
        terms = terms.astype(BF16)
        ones = jnp.ones((16, 128), BF16)
        for g in range(12):
            gcol[b * 12 + g] = dot(terms[:, g * 128:(g + 1) * 128], ones, TN)
    spread[...] = spreading(256)

    pl.semaphore_wait(
        barrier, 31 + has_left.astype(jnp.int32) + has_right.astype(jnp.int32)
        + not_15.astype(jnp.int32) + not_16.astype(jnp.int32))

    def half_copies(s, half):
        left = copy(esend.at[s, 0, half], eright.at[s, half], esem.at[s, 2 * half], ersem.at[s, 2 * half], to_left)
        right = copy(esend.at[s, 1, half], eleft.at[s, half],
                     esem.at[s, 2 * half + 1], ersem.at[s, 2 * half + 1], to_right)
        return left, right

    def half_start(s, half):
        left, right = half_copies(s, half)
        pl.when(has_left)(left.start)
        pl.when(has_right)(right.start)

    def near_wait(left, right):
        pl.when(has_left)(left.wait_send)
        pl.when(has_right)(left.wait_recv)
        pl.when(has_right)(right.wait_send)
        pl.when(has_left)(right.wait_recv)

    def half_wait(s, half):
        near_wait(*half_copies(s, half))

    def edge_copies(s):
        left = copy(esend.at[s, 0], eright.at[s], esem.at[s, 0], ersem.at[s, 0], to_left)
        right = copy(esend.at[s, 1], eleft.at[s], esem.at[s, 1], ersem.at[s, 1], to_right)
        right_m = left_m = None
        if s < 2:
            right_m = copy(esend.at[s, 1, 1], eright_m.at[s], esem.at[s, 2], ersem.at[s, 2], to_right_m)
            left_m = copy(esend.at[s, 0, 1], eleft_m.at[s], esem.at[s, 3], ersem.at[s, 3], to_left_m)
        return left, right, right_m, left_m

    def edges_start(s):
        left, right, right_m, left_m = edge_copies(s)
        pl.when(has_left)(left.start)
        pl.when(has_right)(right.start)
        if s < 2:
            pl.when(not_15)(right_m.start)
            pl.when(not_16)(left_m.start)

            @pl.when(me == 15)
            def _():
                eright_m[s] = esend[s, 1, 1]

            @pl.when(me == 16)
            def _():
                eleft_m[s] = esend[s, 0, 1]

    def edges_wait_near(s):
        left, right, _, _ = edge_copies(s)
        near_wait(left, right)

    def edges_wait_far(s):
        _, _, right_m, left_m = edge_copies(s)
        pl.when(not_15)(right_m.wait)
        pl.when(not_16)(left_m.wait)

    def edges_store(s, half, value):
        esend[s, 0, half] = value[0:16].astype(BF16)
        esend[s, 1, half] = value[16:32].astype(BF16)

    def halo(s, half, slot, mirrored):
        parts = [eright[s, half], eleft[s, half]]
        if mirrored:
            parts += [eright_m[s], eleft_m[s]]
        return dot(jnp.concatenate(parts, axis=0), place[slot, 0:16 * len(parts)], TN)

    def panel(step, g):
        src, dst = ((h0_hbm.at[g + 6], rc0.at[g]), (dzs1.at[g], rc2.at[g]), (dzs0.at[g], rc3.at[g]))[step]
        return copy(src, dst, psend.at[step, g], precv.at[step, g], to_mirror)

    for g in (0, 1):
        panel(0, g).start()

    def shifted(value, tail, sign):
        length = value.shape[1]
        whole = jnp.concatenate([value.astype(BF16), tail.astype(BF16)], axis=1)
        parts = []
        for k in range(5):
            shift = (sign * (2 - k)) % (length + 128)
            parts.append((whole if shift == 0 else pltpu.roll(whole, shift, 1))[:, :length])
        return jnp.concatenate(parts, axis=0)

    rev[...] = reversal(256)
    for i in range(6):
        pick0[i] = edge_pick(i, 256)
        pick1[i] = edge_pick(i, 128)
        place[i] = halo_place(i)

    def inverse_of(total):
        return lax.rsqrt(jnp.sum(total, axis=0, keepdims=True) / CHANNELS + 1e-06)

    def inverse_copy(b):
        src, dst = ((iv0s, iv0r), (iv1s, iv1r))[b]
        return copy(src, dst, ivsem.at[b], ivrsem.at[b], to_mirror)

    def normed(acts, inverse, column, length):
        return ((acts.astype(F32) * inverse) * wide(column, length)).astype(BF16)

    def norm(block, acts, inverse, length, target, pick, s):
        for half in (1, 0):
            def body(i, edge):
                g = half * 6 + i
                value = normed(acts[g], inverse, gcol[block * 12 + g], length)
                target[g] = value
                return edge + dot(pick[i], value, NT)
            edges_store(s, half, run(0, 6, body, jnp.zeros((32, 128), F32), PER))

    h0_load.wait()
    total0 = run(0, 12, lambda g, t: t + fold(jnp.square(h0[g].astype(F32))), jnp.zeros((8, 256), F32), 12)
    inv0 = inverse_of(total0)
    iv0s[...] = jnp.broadcast_to(inv0, (8, 256))
    inverse_copy(0).start()
    norm(0, h0, inv0, 256, nb0, pick0, 0)
    edges_start(0)
    for g in (2, 3):
        panel(0, g).start()

    w_load.wait()

    @pl.loop(0, 12)
    def _(g):
        for b in range(2):
            for k in range(5):
                wtr[b, g, :, k * 128:(k + 1) * 128] = wt_in[b, g, :, k * 128:(k + 1) * 128].T

    edges_wait_near(0)
    for g in (4, 5):
        panel(0, g).start()

    def pooled0(g, stack, acts):
        act, slope = gelu_parts(dot(wt_in[0, g], stack))
        high, low = two_terms(acts.astype(F32) + act)
        return (dot(high, spread[...], NT) + dot(low, spread[...], NT)).astype(BF16), slope

    def conv0(g, value, tail):
        stack = shifted(value, tail, 1)
        s0[g] = stack
        pooled, slope = pooled0(g, stack, h0[g])
        gp0[g] = slope
        h1[g] = pooled
        return fold(jnp.square(pooled.astype(F32)))

    def hi0(i, t):
        g = i + 6
        return t + conv0(g, nb0[g], halo(0, 1, i, False))

    def lo0(g, t):
        panel(0, g).wait()
        theirs = normed(rc0[g], iv0r[0:1, :], gcol[6 + g], 256)
        turned = dot(theirs, rev[...])
        nrev[g] = turned.astype(BF16)
        t = t + conv0(g, nb0[g].astype(F32) + turned, halo(0, 0, g, True))
        tail = dot(jnp.concatenate([eleft_m[0], eright_m[0]], axis=0), place[g, 0:32], TN)
        rc1[g], _ = pooled0(g + 6, shifted(theirs, tail, 1), rc0[g])
        return t

    total1 = run(0, 6, hi0, jnp.zeros((8, 128), F32), PER)
    edges_wait_far(0)
    inverse_copy(0).wait()
    total1 = run(0, 6, lo0, total1, 6)
    inv1 = inverse_of(total1)
    iv1s[...] = jnp.broadcast_to(inv1, (8, 128))
    inverse_copy(1).start()
    norm(1, h1, inv1, 128, nb1, pick1, 1)
    edges_start(1)
    edges_wait_near(1)

    def conv1(g, slot, value, tail):
        stack = shifted(value, tail, 1)
        s1[g] = stack
        act, slope = gelu_parts(dot(wt_in[1, g], stack))
        high, low = two_terms(h1[g].astype(F32) + act)
        half_spread = spread[0:64, 0:128]
        lanes = slice(g * 128, (g + 1) * 128)
        secb[:, lanes] = (dot(half_spread, high, NT) + dot(half_spread, low, NT)).astype(BF16)
        dr = dot(cot[:, lanes], half_spread, TN)
        dr1[g] = dr
        dy = (dr * slope).astype(BF16)
        dyb1[g] = dy
        return dot(pick1[slot], dy, NT)

    def hi1(i, e):
        g = i + 6
        return e + conv1(g, i, nb1[g], halo(1, 1, i, False))

    def lo1(g, e):
        turned = dot(normed(rc1[g], iv1r[0:1, :], gcol[18 + g], 128), rev[0:128, 128:256])
        nrev1[g] = turned.astype(BF16)
        return e + conv1(g, g, nb1[g].astype(F32) + turned, halo(1, 0, g, True))

    def weight_grads(b, dyb, stacks, half):
        def body(i, c):
            g = half * 6 + i
            grad = dot(dyb[g], stacks[g], NT).astype(BF16)
            for j in range(8):
                piece = g * 8 + j
                block = piece // 3
                w[b, block // 16, (block // 4) % 4, block % 4, piece % 3] = grad[j * 16:(j + 1) * 16]
            return c
        run(0, 6, body, 0, PER)

    def spans(half):
        mid = 256 if half else 384
        return pl.ds(0, mid), pl.ds(mid, 640 - mid)

    def first(b, half):
        one, two = spans(half)
        cps = []
        for d in range(1, 4):
            cps.append(copy(w.at[b, half, (x + d) % 4, :, :, :, one], rr.at[b, half, d - 1, :, :, :, one],
                            ss1.at[b, half, 0, d - 1], rs1.at[b, half, 0, d - 1], at_x(d)))
            cps.append(copy(w.at[b, half, :, (y + d) % 4, :, :, two], rr.at[b, half, d - 1, :, :, :, two],
                            ss1.at[b, half, 1, d - 1], rs1.at[b, half, 1, d - 1], at_y(d)))
        return cps

    def second(b, half):
        one, two = spans(half)
        cps = []
        for d in range(1, 4):
            cps.append(copy(pp.at[b, half, (y + d) % 4, :, :, one], qq.at[b, half, d - 1, :, :, one],
                            ss2.at[b, half, 0, d - 1], rs2.at[b, half, 0, d - 1], at_y(d)))
            cps.append(copy(pp.at[b, half, (x + d) % 4, :, :, two], qq.at[b, half, d - 1, :, :, two],
                            ss2.at[b, half, 1, d - 1], rs2.at[b, half, 1, d - 1], at_x(d)))
        return cps

    def third(b):
        return copy(sab.at[b, 1 - z], tz.at[b], ss3.at[b], rs3.at[b], at_z())

    def add_first(b, half):
        one, two = spans(half)
        for cp in first(b, half):
            cp.wait()

        @pl.loop(0, 4)
        def _(k):
            a = w[b, half, x, k, :, :, one].astype(F32)
            c = w[b, half, k, y, :, :, two].astype(F32)
            for d in range(3):
                a += rr[b, half, d, k, :, :, one].astype(F32)
                c += rr[b, half, d, k, :, :, two].astype(F32)
            pp[b, half, k, :, :, one] = a.astype(BF16)
            pp[b, half, k, :, :, two] = c.astype(BF16)
        for cp in second(b, half):
            cp.start()

    def add_second(b, half):
        one, two = spans(half)
        for cp in second(b, half):
            cp.wait()
        a = pp[b, half, y, :, :, one].astype(F32)
        c = pp[b, half, x, :, :, two].astype(F32)
        for d in range(3):
            a += qq[b, half, d, :, :, one].astype(F32)
            c += qq[b, half, d, :, :, two].astype(F32)
        sab[b, half, :, :, one] = a.astype(BF16)
        sab[b, half, :, :, two] = c.astype(BF16)
        pl.when(z != half)(third(b).start)

    def grads_out(b, dyb, stacks, half):
        weight_grads(b, dyb, stacks, half)
        for cp in first(b, half):
            cp.start()

    edges_store(2, 1, run(0, 6, hi1, jnp.zeros((32, 128), F32), 6))
    grads_out(1, dyb1, s1, 1)
    edges_wait_far(1)
    inverse_copy(1).wait()
    edges_store(2, 0, run(0, 6, lo1, jnp.zeros((32, 128), F32), 6))
    edges_start(2)
    sec_store = pltpu.make_async_copy(secb, sec_hbm, lsem.at[2])
    sec_store.start()
    grads_out(1, dyb1, s1, 0)
    edges_wait_near(2)

    def back(b, g, slot, half, s, dyb, length):
        return dot(wtr[b, g], shifted(dyb[g], halo(s, half, slot, False), -1)).astype(BF16)

    def scaled_sum(dn, xhat, row, length):
        weighted = dn * xhat
        column = jnp.sum(weighted, axis=1, keepdims=True)
        return fold(weighted * wide(gcol[row], length)), as_row(column)

    def lo1_back(g, c):
        q, theirs = c
        dz = back(1, g, g, 0, 2, dyb1, 128)
        dzs1[g] = dz
        panel(1, g).start()
        dn = dz.astype(F32)
        dn1[g] = dn
        part = fold(dn * (h1[g].astype(F32) * inv1) * gcol[12 + g])
        return q + part, theirs + fold(dn * nrev1[g].astype(F32))

    zero = jnp.zeros((8, 128), F32)
    q1, theirs1 = run(0, 6, lo1_back, (zero, zero), PER)
    high, low = two_terms(jnp.broadcast_to(jnp.sum(theirs1, axis=0, keepdims=True), (16, 128)))
    flip = rev[0:128, 128:256]
    qs[...] = dot(high, flip) + dot(low, flip)
    q_copy = copy(qs, qr, qsem.at[0], qrsem.at[0], to_mirror)
    q_copy.start()

    def hi1_own(g, q):
        dn = back(1, g, g - 6, 1, 2, dyb1, 128).astype(F32)
        dn1[g] = dn
        return q + fold(dn * (h1[g].astype(F32) * inv1) * gcol[12 + g])

    q1 = run(6, 12, hi1_own, q1, PER)
    add_first(1, 1)
    q_copy.wait()
    mean1 = (jnp.sum(q1, axis=0, keepdims=True) + qr[0:1, :]) / CHANNELS

    def grad_mid(half):
        def step(i, e):
            g = half * 6 + i
            dn = dn1[g]
            xhat = h1[g].astype(F32) * inv1
            if half:
                panel(1, i).wait()
                dn = dn + dot(rc2[i], rev[0:128, 128:256])
                dn1[g] = dn
            dh = (dn * gcol[12 + g] - xhat * mean1) * inv1 + dr1[g]
            high, low = two_terms(dh)
            dr = dot(high, spread[...]) + dot(low, spread[...])
            dr0[g] = dr
            dy = (dr * gp0[g]).astype(BF16)
            dyb0[g] = dy
            return e + dot(pick0[i], dy, NT)
        edges_store(3, half, run(0, 6, step, jnp.zeros((32, 128), F32), 6))
        half_start(3, half)
        grads_out(0, dyb0, s0, half)

    grad_mid(0)
    add_first(1, 0)
    grad_mid(1)

    def gains1(g, c):
        dgb[pl.ds(12 + g, 1), :] = as_row(jnp.sum(dn1[g] * (h1[g].astype(F32) * inv1), axis=1, keepdims=True))
        return c

    run(0, 12, gains1, 0, PER)
    half_wait(3, 0)

    def lo0_back(g, q):
        dz = back(0, g, g, 0, 3, dyb0, 256)
        dzs0[g] = dz
        panel(2, g).start()
        dn = dz.astype(F32)
        dn0[g] = dn
        part, row = scaled_sum(dn, h0[g].astype(F32) * inv0, g, 256)
        dgb[pl.ds(g, 1), :] = row
        column = jnp.sum(dn * nrev[g].astype(F32), axis=1, keepdims=True) / gcol[6 + g]
        dgb[pl.ds(6 + g, 1), :] = as_row(column)
        return q + part

    q0 = run(0, 6, lo0_back, jnp.zeros((8, 256), F32), PER)

    half_wait(3, 1)

    def hi0_own(g, c):
        dn = back(0, g, g - 6, 1, 3, dyb0, 256).astype(F32)
        dn0[g] = dn
        column = jnp.sum(dn * (h0[g].astype(F32) * inv0), axis=1, keepdims=True)
        dgb[pl.ds(g, 1), :] += as_row(column)
        return c

    run(6, 12, hi0_own, 0, PER)

    gbuf[0] = dgb[...]
    gx = [copy(gbuf.at[0], g1.at[d - 1], sg.at[0, d - 1], rg.at[0, d - 1], at_x(d)) for d in range(1, 4)]
    gy = [copy(gbuf.at[1], g2.at[d - 1], sg.at[1, d - 1], rg.at[1, d - 1], at_y(d)) for d in range(1, 4)]
    gz = copy(gbuf.at[2], g3, sg.at[2, 0], rg.at[2, 0], at_z())
    for cp in gx:
        cp.start()
    add_second(1, 1)
    add_second(1, 0)
    add_first(0, 0)
    for cp in gx:
        cp.wait()
    gbuf[1] = gbuf[0] + g1[0] + g1[1] + g1[2]
    for cp in gy:
        cp.start()
    add_first(0, 1)
    add_second(0, 0)
    for cp in gy:
        cp.wait()
    gbuf[2] = gbuf[1] + g2[0] + g2[1] + g2[2]
    gz.start()

    add_second(0, 1)
    gz.wait()
    total_g = gbuf[2] + g3[...]
    square = jnp.sum(total_g * total_g) * (1.0 / 32.0)
    for b in (1, 0):
        third(b).wait()
        full = sab[b, z].astype(F32) + tz[b].astype(F32)
        out[b] = full
        square += jnp.sum(full * full)
    sq[0] = jnp.full((8, 128), square, F32)
    near = [copy(sq.at[0], sq1.at[d - 1], sn.at[0], rn.at[0], at_plane(d)) for d in range(1, 16)]
    for cp in near:
        cp.start()

    def hi0_back(i, q):
        g = i + 6
        panel(2, i).wait()
        dn = dn0[g] + dot(rc3[i], rev[...])
        dn0[g] = dn
        xhat = h0[g].astype(F32) * inv0
        return q + fold(dn * xhat * wide(gcol[g], 256))

    q0 = run(0, 6, hi0_back, q0, 6)
    mean0 = jnp.sum(q0, axis=0, keepdims=True) / CHANNELS

    def finish(g, c):
        xhat = h0[g].astype(F32) * inv0
        igb[g] = ((dn0[g] * wide(gcol[g], 256) - xhat * mean0) * inv0 + dr0[g]).astype(BF16)
        return c

    run(0, 12, finish, 0, PER)
    ig_store = pltpu.make_async_copy(igb, ig_hbm, lsem.at[3])
    ig_store.start()
    copy(sq1, sq1, sn.at[0], rn.at[0], to_mirror).wait()
    sq[1] = sq[0] + jnp.sum(sq1[...], axis=0)
    far = [copy(sq.at[1], sq2.at[d - 1], sn.at[1], rn.at[1], at_line(d)) for d in range(1, 16)]
    for cp in far:
        cp.start()
    copy(sq2, sq2, sn.at[1], rn.at[1], to_mirror).wait()
    total = sq[1] + jnp.sum(sq2[...], axis=0)
    factor = jnp.minimum(1.0, lax.rsqrt(total / COUNT + 1e-06))[0:1, 0:1]
    for b in range(2):
        out[b] = out[b] * factor
    gfull[...] = total_g * factor
    start = me * 48
    for b in range(2):
        row = b * 12 + start // 128
        pair = jnp.concatenate([gfull[pl.ds(row, 1), :], gfull[pl.ds(row + 1, 1), :]], axis=1)
        pair = pltpu.roll(jnp.broadcast_to(pair, (8, 256)), (256 - start % 128) % 256, 1)
        gout[b:b + 1, :] = pair[0:1, 0:48]
    sec_store.wait()
    ig_store.wait()


def hand_on(*refs):
    count = len(refs) // 2
    for source, target in zip(refs[:count], refs[count:]):
        target[...] = source[...]


def local(section_input, out_cotangent, conv_weight, norm_gain):
    h0 = section_input.reshape(12, 128, 256)
    cot = out_cotangent[0].T
    weights = conv_weight.reshape(2, 12, 128, 640)
    gain = norm_gain[0]
    dma = pltpu.SemaphoreType.DMA

    def vm(shape, kind=BF16):
        return pltpu.VMEM(shape, kind)

    hbm = pl.BlockSpec(memory_space=pl.ANY)
    vmem = pl.BlockSpec(memory_space=pltpu.VMEM)
    second, grad_in, wshare, gshare = pl.pallas_call(
        kernel,
        out_shape=(
            jax.ShapeDtypeStruct((64, 1536), BF16),
            jax.ShapeDtypeStruct((12, 128, 256), BF16),
            jax.ShapeDtypeStruct((2, 3, 16, 640), F32),
            jax.ShapeDtypeStruct((2, 48), F32),
        ),
        in_specs=[hbm, vmem, hbm, vmem],
        out_specs=[hbm, hbm, vmem, vmem],
        scratch_shapes=[
            vm((12, 128, 256)), vm((2, 12, 128, 640)), vm((64, 1536)), vm((12, 128, 256)),
            vm((256, 256)), vm((128, 256)), vm((6, 32, 256)), vm((6, 32, 128)), vm((6, 64, 128)),
            vm((8, 256), F32), vm((8, 128), F32), vm((8, 256), F32), vm((8, 128), F32), vm((32, 128), F32),
            vm((24, 128, 128), F32), vm((2, 12, 128, 640)),
            vm((12, 128, 256)), vm((12, 128, 128)), vm((12, 128, 128)),
            vm((12, 640, 256)), vm((12, 640, 128)),
            vm((12, 128, 256), F32), vm((12, 128, 256), F32), vm((12, 128, 128), F32),
            vm((12, 128, 256)), vm((12, 128, 128)),
            vm((12, 128, 256), F32), vm((12, 128, 128), F32),
            vm((6, 128, 256)), vm((6, 128, 128)), vm((6, 128, 256)),
            vm((6, 128, 256)), vm((6, 128, 128)), vm((6, 128, 128)), vm((6, 128, 256)),
            vm((4, 2, 2, 16, 128)), vm((4, 2, 16, 128)), vm((4, 2, 16, 128)),
            vm((2, 16, 128)), vm((2, 16, 128)), vm((32, 128), F32),
            vm((2, 2, 4, 4, 3, 16, 640)), vm((2, 2, 3, 4, 3, 16, 640)),
            vm((2, 2, 4, 3, 16, 640)), vm((2, 2, 3, 3, 16, 640)),
            vm((2, 2, 3, 16, 640)), vm((2, 3, 16, 640)),
            vm((6, 128, 128)), vm((16, 128), F32), vm((16, 128), F32),
            vm((3, 32, 128), F32), vm((3, 32, 128), F32), vm((3, 32, 128), F32), vm((32, 128), F32),
            vm((2, 8, 128), F32), vm((15, 8, 128), F32), vm((15, 8, 128), F32),
            dma((3, 6)), dma((3, 6)), dma((4, 4)), dma((4, 4)), dma((2,)), dma((2,)), dma((4,)), dma((1,)), dma((1,)),
            dma((2, 2, 2, 3)), dma((2, 2, 2, 3)), dma((2, 2, 2, 3)), dma((2, 2, 2, 3)), dma((2,)), dma((2,)),
            dma((3, 3)), dma((3, 3)), dma((2,)), dma((2,)),
        ],
        compiler_params=pltpu.CompilerParams(
            collective_id=0, has_side_effects=True, vmem_limit_bytes=56 << 20),
        name="tower",
    )(h0, cot, weights, gain)
    second, grad_in, wshare, gshare = pl.pallas_call(
        hand_on,
        out_shape=[jax.ShapeDtypeStruct(a.shape, a.dtype) for a in (second, grad_in, wshare, gshare)],
        in_specs=[vmem] * 4,
        out_specs=[vmem] * 4,
        name="hand_on",
    )(second, grad_in, wshare, gshare)
    return (
        second.T[None],
        grad_in.reshape(1, 1536, 256),
        wshare.reshape(1, 2, 48, 640),
        gshare[None],
    )


def solution(mesh):
    placed = (
        P("section", None, "ctx"),
        P("section", None, "ctx"),
        P("section", None, None, None),
        P("section", None, None),
    )
    return jax.shard_map(
        local,
        mesh=mesh,
        in_specs=placed,
        out_specs=(
            P("section", None, "ctx"),
            P("section", None, "ctx"),
            P("section", None, "ctx", None),
            P("section", None, "ctx"),
        ),
        check_vma=False,
    )
```

time: 137 us -> 116 us (0.85)
  Pallas kernels: 126 us -> 115 us
  local copies, waits for them, and re-layouts: 10.1 us -> 0 us
    pallas_call x1 -> x2, Pallas kernels: 126 us -> 115 us  [the longest x1 113 us: local(): pl.pallas_call(kernel, out_shape=(jax.ShapeDtypeStruct((64, 1536), BF16),...]
    unnamed x4 -> x0, local copies, waits for them, and re-layouts: 7.39 us -> none
where the time goes in v3:
time: 116 us
  Pallas kernels  115 us (99%)
    pallas_call x1, Pallas kernels, local(): pl.pallas_call(kernel, out_shape=(jax.ShapeDtypeStruct((64, 1536), BF16),...  113 us

profile of v3, /device:TPU:1, one launch (start us, length us, event | category | flops | bytes accessed | tf_op | source)
XLA Modules:
  0.0 115.8 jit_solution(13862142708506289827)
XLA Ops:
  0.6 112.8 %tower.1 = (bf16[64,1536]{1,0:T(8,128)(2,1)}, bf16[12,128,256]{2,1,0:T(8,128)(2,1)}, f32[2,3,16,640]{3,2,1,0:T(8,128)}, f32[2,48]{1,0:T(2,128)}) custom-call(bf16[12,128,256]{2,1,0:T(8,128)(2,1)} %bitcast.13, bf16[64,1536]{1,0:T(8,128)(2,1)} %bitcast.14, bf16[2,12,128,640]{3,2,1,0:T(8,128)(2,1)} %bitcast.12, f32[2,1536]{1,0:T(2,128)} %bitcast.15), custom_call_target="tpu_custom_call" | custom-call | tf_op jit(solution)/shard_map/tower/pallas_call | solution.py:661
  113.4 2.3 %hand_on.1 = (bf16[64,1536]{1,0:T(8,128)(2,1)}, bf16[12,128,256]{2,1,0:T(8,128)(2,1)}, f32[2,3,16,640]{3,2,1,0:T(8,128)}, f32[2,48]{1,0:T(2,128)}) custom-call(bf16[64,1536]{1,0:T(8,128)(2,1)} %get-tuple-element.12.refs_0_, bf16[12,128,256]{2,1,0:T(8,128)(2,1)} %get-tuple-element.13.refs_1_, f32[2,3,16,640]{3,2,1,0:T(8,128)} %get-tuple-element.14.refs_2_, ...), custom_call_target="tpu_custom_call" | custom-call | tf_op jit(solution)/shard_map/hand_on/pallas_call | solution.py:699

commit v4 on v3

--- a/solution.py
+++ b/solution.py
@@ -195,7 +195,8 @@
         ones = jnp.ones((16, 128), BF16)
         for g in range(12):
             gcol[b * 12 + g] = dot(terms[:, g * 128:(g + 1) * 128], ones, TN)
-    spread[...] = spreading(256)
+    spread[0:128] = spreading(256)
+    spread[128:256] = spreading(256)
 
     pl.semaphore_wait(
         barrier, 31 + has_left.astype(jnp.int32) + has_right.astype(jnp.int32)
@@ -303,8 +304,17 @@
                 g = half * 6 + i
                 value = normed(acts[g], inverse, gcol[block * 12 + g], length)
                 target[g] = value
-                return edge + dot(pick[i], value, NT)
-            edges_store(s, half, run(0, 6, body, jnp.zeros((32, 128), F32), PER))
+                return edge + dot(pick[i], value, NT) if length == 256 else edge
+            edge = run(0, 6, body, jnp.zeros((32, 128), F32), PER)
+            edges_store(s, half, edge if length == 256 else paired_edges(target, half))
+
+    def paired_edges(source, half):
+        edge = jnp.zeros((32, 128), F32)
+        for i in (0, 2, 4):
+            g = half * 6 + i
+            edge += dot(jnp.concatenate([pick1[i], pick1[i + 1]], axis=1),
+                        jnp.concatenate([source[g], source[g + 1]], axis=1), NT)
+        return edge
 
     h0_load.wait()
     total0 = run(0, 12, lambda g, t: t + fold(jnp.square(h0[g].astype(F32))), jnp.zeros((8, 256), F32), 12)
@@ -324,6 +334,7 @@
             for k in range(5):
                 wtr[b, g, :, k * 128:(k + 1) * 128] = wt_in[b, g, :, k * 128:(k + 1) * 128].T
 
+    dr1[...] = dot(cot[...], spread[0:64, 0:128], TN).reshape(12, 128, 128)
     edges_wait_near(0)
     for g in (4, 5):
         panel(0, g).start()
@@ -331,7 +342,7 @@
     def pooled0(g, stack, acts):
         act, slope = gelu_parts(dot(wt_in[0, g], stack))
         high, low = two_terms(acts.astype(F32) + act)
-        return (dot(high, spread[...], NT) + dot(low, spread[...], NT)).astype(BF16), slope
+        return (dot(high, spread[0:128], NT) + dot(low, spread[0:128], NT)).astype(BF16), slope
 
     def conv0(g, value, tail):
         stack = shifted(value, tail, 1)
@@ -347,18 +358,23 @@
 
     def lo0(g, t):
         panel(0, g).wait()
-        theirs = normed(rc0[g], iv0r[0:1, :], gcol[6 + g], 256)
-        turned = dot(theirs, rev[...])
-        nrev[g] = turned.astype(BF16)
-        t = t + conv0(g, nb0[g].astype(F32) + turned, halo(0, 0, g, True))
-        tail = dot(jnp.concatenate([eleft_m[0], eright_m[0]], axis=0), place[g, 0:32], TN)
-        rc1[g], _ = pooled0(g + 6, shifted(theirs, tail, 1), rc0[g])
+        panel(0, g + 1).wait()
+        both = jnp.concatenate(
+            [normed(rc0[k], iv0r[0:1, :], gcol[6 + k], 256) for k in (g, g + 1)], axis=0)
+        turned = dot(both, rev[...])
+        for k in (g, g + 1):
+            rows = slice((k - g) * 128, (k - g + 1) * 128)
+            nrev[k] = turned[rows].astype(BF16)
+            t = t + conv0(k, nb0[k].astype(F32) + turned[rows], halo(0, 0, k, True))
+            tail = dot(jnp.concatenate([eleft_m[0], eright_m[0]], axis=0), place[k, 0:32], TN)
+            rc1[k], _ = pooled0(k + 6, shifted(both[rows], tail, 1), rc0[k])
         return t
 
     total1 = run(0, 6, hi0, jnp.zeros((8, 128), F32), PER)
     edges_wait_far(0)
     inverse_copy(0).wait()
-    total1 = run(0, 6, lo0, total1, 6)
+    for g in (0, 2, 4):
+        total1 = lo0(g, total1)
     inv1 = inverse_of(total1)
     iv1s[...] = jnp.broadcast_to(inv1, (8, 128))
     inverse_copy(1).start()
@@ -366,28 +382,15 @@
     edges_start(1)
     edges_wait_near(1)
 
-    def conv1(g, slot, value, tail):
+    def conv1(g, value, tail):
         stack = shifted(value, tail, 1)
         s1[g] = stack
         act, slope = gelu_parts(dot(wt_in[1, g], stack))
-        high, low = two_terms(h1[g].astype(F32) + act)
+        terms = jnp.concatenate(two_terms(h1[g].astype(F32) + act), axis=1)
         half_spread = spread[0:64, 0:128]
-        lanes = slice(g * 128, (g + 1) * 128)
-        secb[:, lanes] = (dot(half_spread, high, NT) + dot(half_spread, low, NT)).astype(BF16)
-        dr = dot(cot[:, lanes], half_spread, TN)
-        dr1[g] = dr
-        dy = (dr * slope).astype(BF16)
-        dyb1[g] = dy
-        return dot(pick1[slot], dy, NT)
-
-    def hi1(i, e):
-        g = i + 6
-        return e + conv1(g, i, nb1[g], halo(1, 1, i, False))
-
-    def lo1(g, e):
-        turned = dot(normed(rc1[g], iv1r[0:1, :], gcol[18 + g], 128), rev[0:128, 128:256])
-        nrev1[g] = turned.astype(BF16)
-        return e + conv1(g, g, nb1[g].astype(F32) + turned, halo(1, 0, g, True))
+        pooled = dot(jnp.concatenate([half_spread, half_spread], axis=1), terms, NT)
+        secb[:, g * 128:(g + 1) * 128] = pooled.astype(BF16)
+        dyb1[g] = (dr1[g] * slope).astype(BF16)
 
     def weight_grads(b, dyb, stacks, half):
         def body(i, c):
@@ -462,15 +465,27 @@
         for cp in first(b, half):
             cp.start()
 
-    edges_store(2, 1, run(0, 6, hi1, jnp.zeros((32, 128), F32), 6))
+    for i in range(6):
+        conv1(i + 6, nb1[i + 6], halo(1, 1, i, False))
+    edges_store(2, 1, paired_edges(dyb1, 1))
+    distant = jnp.logical_or(me == 15, me == 16)
+
     grads_out(1, dyb1, s1, 1)
+
     edges_wait_far(1)
     inverse_copy(1).wait()
-    edges_store(2, 0, run(0, 6, lo1, jnp.zeros((32, 128), F32), 6))
+    theirs = jnp.concatenate([normed(rc1[g], iv1r[0:1, :], gcol[18 + g], 128) for g in range(6)], axis=0)
+    turned = dot(theirs, rev[0:128, 128:256])
+    for g in range(6):
+        part = turned[g * 128:(g + 1) * 128]
+        nrev1[g] = part.astype(BF16)
+        conv1(g, nb1[g].astype(F32) + part, halo(1, 0, g, True))
+    edges_store(2, 0, paired_edges(dyb1, 0))
     edges_start(2)
     sec_store = pltpu.make_async_copy(secb, sec_hbm, lsem.at[2])
     sec_store.start()
     grads_out(1, dyb1, s1, 0)
+
     edges_wait_near(2)
 
     def back(b, g, slot, half, s, dyb, length):
@@ -485,7 +500,6 @@
         q, theirs = c
         dz = back(1, g, g, 0, 2, dyb1, 128)
         dzs1[g] = dz
-        panel(1, g).start()
         dn = dz.astype(F32)
         dn1[g] = dn
         part = fold(dn * (h1[g].astype(F32) * inv1) * gcol[12 + g])
@@ -498,6 +512,8 @@
     qs[...] = dot(high, flip) + dot(low, flip)
     q_copy = copy(qs, qr, qsem.at[0], qrsem.at[0], to_mirror)
     q_copy.start()
+    for g in range(3):
+        panel(1, g).start()
 
     def hi1_own(g, q):
         dn = back(1, g, g - 6, 1, 2, dyb1, 128).astype(F32)
@@ -505,22 +521,27 @@
         return q + fold(dn * (h1[g].astype(F32) * inv1) * gcol[12 + g])
 
     q1 = run(6, 12, hi1_own, q1, PER)
+    for g in range(3, 6):
+        panel(1, g).start()
     add_first(1, 1)
     q_copy.wait()
     mean1 = (jnp.sum(q1, axis=0, keepdims=True) + qr[0:1, :]) / CHANNELS
 
     def grad_mid(half):
+        if half:
+            for i in range(6):
+                panel(1, i).wait()
+            turned = dot(rc2[...].reshape(768, 128), rev[0:128, 128:256])
+
         def step(i, e):
             g = half * 6 + i
             dn = dn1[g]
             xhat = h1[g].astype(F32) * inv1
             if half:
-                panel(1, i).wait()
-                dn = dn + dot(rc2[i], rev[0:128, 128:256])
+                dn = dn + turned[i * 128:(i + 1) * 128]
                 dn1[g] = dn
             dh = (dn * gcol[12 + g] - xhat * mean1) * inv1 + dr1[g]
-            high, low = two_terms(dh)
-            dr = dot(high, spread[...]) + dot(low, spread[...])
+            dr = dot(jnp.concatenate(two_terms(dh), axis=1), spread[...])
             dr0[g] = dr
             dy = (dr * gp0[g]).astype(BF16)
             dyb0[g] = dy
@@ -543,7 +564,8 @@
     def lo0_back(g, q):
         dz = back(0, g, g, 0, 3, dyb0, 256)
         dzs0[g] = dz
-        panel(2, g).start()
+        if g < 2:
+            panel(2, g).start()
         dn = dz.astype(F32)
         dn0[g] = dn
         part, row = scaled_sum(dn, h0[g].astype(F32) * inv0, g, 256)
@@ -565,6 +587,8 @@
 
     run(6, 12, hi0_own, 0, PER)
 
+    for g in (2, 3):
+        panel(2, g).start()
     gbuf[0] = dgb[...]
     gx = [copy(gbuf.at[0], g1.at[d - 1], sg.at[0, d - 1], rg.at[0, d - 1], at_x(d)) for d in range(1, 4)]
     gy = [copy(gbuf.at[1], g2.at[d - 1], sg.at[1, d - 1], rg.at[1, d - 1], at_y(d)) for d in range(1, 4)]
@@ -574,6 +598,8 @@
     add_second(1, 1)
     add_second(1, 0)
     add_first(0, 0)
+    for g in (4, 5):
+        panel(2, g).start()
     for cp in gx:
         cp.wait()
     gbuf[1] = gbuf[0] + g1[0] + g1[1] + g1[2]
@@ -600,6 +626,11 @@
     for cp in near:
         cp.start()
 
+    copy(sq1, sq1, sn.at[0], rn.at[0], to_mirror).wait()
+    sq[1] = sq[0] + jnp.sum(sq1[...], axis=0)
+    far = [copy(sq.at[1], sq2.at[d - 1], sn.at[1], rn.at[1], at_line(d)) for d in range(1, 16)]
+    for cp in far:
+        cp.start()
     def hi0_back(i, q):
         g = i + 6
         panel(2, i).wait()
@@ -619,11 +650,6 @@
     run(0, 12, finish, 0, PER)
     ig_store = pltpu.make_async_copy(igb, ig_hbm, lsem.at[3])
     ig_store.start()
-    copy(sq1, sq1, sn.at[0], rn.at[0], to_mirror).wait()
-    sq[1] = sq[0] + jnp.sum(sq1[...], axis=0)
-    far = [copy(sq.at[1], sq2.at[d - 1], sn.at[1], rn.at[1], at_line(d)) for d in range(1, 16)]
-    for cp in far:
-        cp.start()
     copy(sq2, sq2, sn.at[1], rn.at[1], to_mirror).wait()
     total = sq[1] + jnp.sum(sq2[...], axis=0)
     factor = jnp.minimum(1.0, lax.rsqrt(total / COUNT + 1e-06))[0:1, 0:1]
@@ -670,7 +696,7 @@
         out_specs=[hbm, hbm, vmem, vmem],
         scratch_shapes=[
             vm((12, 128, 256)), vm((2, 12, 128, 640)), vm((64, 1536)), vm((12, 128, 256)),
-            vm((256, 256)), vm((128, 256)), vm((6, 32, 256)), vm((6, 32, 128)), vm((6, 64, 128)),
+            vm((256, 256)), vm((256, 256)), vm((6, 32, 256)), vm((6, 32, 128)), vm((6, 64, 128)),
             vm((8, 256), F32), vm((8, 128), F32), vm((8, 256), F32), vm((8, 128), F32), vm((32, 128), F32),
             vm((24, 128, 128), F32), vm((2, 12, 128, 640)),
             vm((12, 128, 256)), vm((12, 128, 128)), vm((12, 128, 128)),

time: 116 us -> 112 us (0.966)
  Pallas kernels: 115 us -> 111 us
    pallas_call x1, Pallas kernels: 113 us -> 109 us  [local(): pl.pallas_call(kernel, out_shape=(jax.ShapeDtypeStruct((64, 1536), BF16),...]
where the time goes in v4:
time: 112 us
  Pallas kernels  111 us (99%)
    pallas_call x1, Pallas kernels, local(): pl.pallas_call(kernel, out_shape=(jax.ShapeDtypeStruct((64, 1536), BF16),...  109 us
    pallas_call x1, Pallas kernels, local(): pl.pallas_call(hand_on, out_shape=[jax.ShapeDtypeStruct(a.shape, a.dtype)...  2.31 us

profile of v4, /device:TPU:1, one launch (start us, length us, event | category | flops | bytes accessed | tf_op | source)
XLA Modules:
  0.0 111.9 jit_solution(17862309660602770962)
XLA Ops:
  0.6 108.9 %tower.1 = (bf16[64,1536]{1,0:T(8,128)(2,1)}, bf16[12,128,256]{2,1,0:T(8,128)(2,1)}, f32[2,3,16,640]{3,2,1,0:T(8,128)}, f32[2,48]{1,0:T(2,128)}) custom-call(bf16[12,128,256]{2,1,0:T(8,128)(2,1)} %bitcast.13, bf16[64,1536]{1,0:T(8,128)(2,1)} %bitcast.14, bf16[2,12,128,640]{3,2,1,0:T(8,128)(2,1)} %bitcast.12, f32[2,1536]{1,0:T(2,128)} %bitcast.15), custom_call_target="tpu_custom_call" | custom-call | tf_op jit(solution)/shard_map/tower/pallas_call | solution.py:687
  109.6 2.3 %hand_on.1 = (bf16[64,1536]{1,0:T(8,128)(2,1)}, bf16[12,128,256]{2,1,0:T(8,128)(2,1)}, f32[2,3,16,640]{3,2,1,0:T(8,128)}, f32[2,48]{1,0:T(2,128)}) custom-call(bf16[64,1536]{1,0:T(8,128)(2,1)} %get-tuple-element.12.refs_0_, bf16[12,128,256]{2,1,0:T(8,128)(2,1)} %get-tuple-element.13.refs_1_, f32[2,3,16,640]{3,2,1,0:T(8,128)} %get-tuple-element.14.refs_2_, ...), custom_call_target="tpu_custom_call" | custom-call | tf_op jit(solution)/shard_map/hand_on/pallas_call | solution.py:725

commit v5 on v4

--- a/solution.py
+++ b/solution.py
@@ -470,10 +470,12 @@
     edges_store(2, 1, paired_edges(dyb1, 1))
     distant = jnp.logical_or(me == 15, me == 16)
 
-    grads_out(1, dyb1, s1, 1)
+    weight_grads(1, dyb1, s1, 1)
 
     edges_wait_far(1)
     inverse_copy(1).wait()
+    for cp in first(1, 1):
+        cp.start()
     theirs = jnp.concatenate([normed(rc1[g], iv1r[0:1, :], gcol[18 + g], 128) for g in range(6)], axis=0)
     turned = dot(theirs, rev[0:128, 128:256])
     for g in range(6):

time: 112 us -> 112 us (level)
  no operation moved by 1% of the time
where the time goes in v5:
time: 112 us; the launch traced here: 111 us
  Pallas kernels  111 us (99%)
    pallas_call x1, Pallas kernels, local(): pl.pallas_call(kernel, out_shape=(jax.ShapeDtypeStruct((64, 1536), BF16),...  108 us
    pallas_call x1, Pallas kernels, local(): pl.pallas_call(hand_on, out_shape=[jax.ShapeDtypeStruct(a.shape, a.dtype)...  2.31 us

profile of v5, /device:TPU:1, one launch (start us, length us, event | category | flops | bytes accessed | tf_op | source)
XLA Modules:
  0.0 111.4 jit_solution(10496704757829011023)
XLA Ops:
  0.6 108.4 %tower.1 = (bf16[64,1536]{1,0:T(8,128)(2,1)}, bf16[12,128,256]{2,1,0:T(8,128)(2,1)}, f32[2,3,16,640]{3,2,1,0:T(8,128)}, f32[2,48]{1,0:T(2,128)}) custom-call(bf16[12,128,256]{2,1,0:T(8,128)(2,1)} %bitcast.13, bf16[64,1536]{1,0:T(8,128)(2,1)} %bitcast.14, bf16[2,12,128,640]{3,2,1,0:T(8,128)(2,1)} %bitcast.12, f32[2,1536]{1,0:T(2,128)} %bitcast.15), custom_call_target="tpu_custom_call" | custom-call | tf_op jit(solution)/shard_map/tower/pallas_call | solution.py:689
  109.1 2.3 %hand_on.1 = (bf16[64,1536]{1,0:T(8,128)(2,1)}, bf16[12,128,256]{2,1,0:T(8,128)(2,1)}, f32[2,3,16,640]{3,2,1,0:T(8,128)}, f32[2,48]{1,0:T(2,128)}) custom-call(bf16[64,1536]{1,0:T(8,128)(2,1)} %get-tuple-element.12.refs_0_, bf16[12,128,256]{2,1,0:T(8,128)(2,1)} %get-tuple-element.13.refs_1_, f32[2,3,16,640]{3,2,1,0:T(8,128)} %get-tuple-element.14.refs_2_, ...), custom_call_target="tpu_custom_call" | custom-call | tf_op jit(solution)/shard_map/hand_on/pallas_call | solution.py:727
